TPU v7x, 512 devices: a whole 4x4x16 slice. The times are simulated.
512 devices in a mesh: wide: 32 (over z, core), narrow: 16 (over y, x).
Axes of the slice: x: 4, y: 4, z: 16, core: 2. Of those that a mesh axis runs over, the one named last changes fastest.
Arguments:
- vectors: bfloat16 [64, 2097152], P(None, ('wide', 'narrow'))
- anchors: float32 [2097152], P(('wide', 'narrow')), may hold values from 0.5 to 4
- pins: int32 [8, 2621440], P(None, ('wide', 'narrow')), may hold values from -1 to 6143, as said below
- halo_rows: int32 [2, 524288], P(None, ('wide', 'narrow')), may hold values from 0 to 4095, as said below
Outputs:
- embedding: float32 [64, 2097152], P(None, ('wide', 'narrow'))
- r_factor: float32 [64, 64], replicated
Inputs may be any that keep to these rules, and one draw needn't show every extreme that they name: Each net lists 2 to 8 valid pins first, then -1; the first net of every partition has 8 pins and the second 2; pins index the extended list of the net's own partition, and the first net of every partition names its last entry. `halo_rows`: each partition's list for each direction holds 1024 distinct rows of that partition.
All inputs are finite; a program needn't handle non-finite values.
Results may differ from a plain program's by a relative error of at most 0.00096.
Values may be sent and summed in bfloat16 or wider, within the bound.
No kernel may reach another device: no remote copies, remote signals or barrier semaphores. Data moves between devices by JAX's collectives and lax.ppermute only.
A program may use at most 64 MiB of HBM per device.

v0:
```python
import math

import jax
import jax.numpy as jnp
from jax import lax
from jax.sharding import PartitionSpec as P


def shifted(value, axis, steps):
    count = lax.axis_size(axis)
    pairs = [(source, (source + steps) % count) for source in range(count)]
    return lax.ppermute(value, axis, pairs)


def factorize(gram):
    width = gram.shape[0]
    places = lax.broadcasted_iota(jnp.int32, (width,), 0)

    def one_column(index, carry):
        rest, lower = carry
        unit = (places == index).astype(jnp.float32)
        column = jnp.dot(
            rest, unit, precision=lax.Precision.HIGHEST, preferred_element_type=jnp.float32
        )
        pivot = jnp.sum(column * unit)
        column = jnp.where(places >= index, column, 0.0) / jnp.sqrt(pivot)
        rest = rest - column[:, None] * column[None, :]
        lower = lower + column[:, None] * unit[None, :]
        return (rest, lower)

    start = (gram, jnp.zeros((width, width), jnp.float32))
    _, lower = lax.fori_loop(0, width, one_column, start)
    return lower.T


def invert_upper(factor):
    width = factor.shape[0]
    places = lax.broadcasted_iota(jnp.int32, (width,), 0)

    def one_row(step, solved):
        index = width - 1 - step
        unit = (places == index).astype(jnp.float32)
        row = jnp.dot(
            unit, factor, precision=lax.Precision.HIGHEST, preferred_element_type=jnp.float32
        )
        pivot = jnp.sum(row * unit)
        known = jnp.dot(
            row, solved, precision=lax.Precision.HIGHEST, preferred_element_type=jnp.float32
        )
        fresh = (unit - known) / pivot
        return solved + unit[:, None] * fresh[None, :]

    return lax.fori_loop(0, width, one_row, jnp.zeros((width, width), jnp.float32))


def body(vectors, anchors, pins, halo_rows):
    cells = vectors.shape[1]
    up_list = halo_rows[0]
    down_list = halo_rows[1]
    prev_block, prev_list = shifted((vectors, up_list), ("wide", "narrow"), 1)
    next_block, next_list = shifted((vectors, down_list), ("wide", "narrow"), -1)
    from_prev = jnp.take(prev_block, prev_list, axis=1)
    from_next = jnp.take(next_block, next_list, axis=1)
    extended = jnp.concatenate([vectors, from_prev, from_next], axis=1)
    total = extended.shape[1]
    width = vectors.shape[0]
    slots = pins.shape[0]
    nets = pins.shape[1]
    block = math.gcd(nets, 512)
    pin_blocks = pins.reshape(slots, nets // block, block).transpose(1, 0, 2)
    column = lax.broadcasted_iota(jnp.int32, (1, total), 1)

    def one_block(carry, pin_block):
        contrib, degree = carry
        incidence = jnp.zeros((block, total), jnp.bfloat16)
        for slot in range(slots):
            incidence = incidence + (pin_block[slot][:, None] == column).astype(jnp.bfloat16)
        size = jnp.sum((pin_block >= 0).astype(jnp.float32), axis=0)
        weight = 1.0 / (size - 1.0)
        sums = lax.dot_general(
            extended, incidence, (((1,), (1,)), ((), ())), preferred_element_type=jnp.float32
        )
        scaled = (sums * weight[None, :]).astype(jnp.bfloat16)
        local = incidence[:, :cells]
        contrib = contrib + jnp.dot(scaled, local, preferred_element_type=jnp.float32)
        degree = (
            degree
            + jnp.dot(
                (weight * size)[None, :],
                local.astype(jnp.float32),
                precision=lax.Precision.HIGHEST,
                preferred_element_type=jnp.float32,
            )[0]
        )
        return ((contrib, degree), None)

    start = (jnp.zeros((width, cells), jnp.float32), jnp.zeros((cells,), jnp.float32))
    (contrib, degree), _ = lax.scan(one_block, start, pin_blocks)
    image = (degree + anchors)[None, :] * vectors.astype(jnp.float32) - contrib
    partial_gram = jnp.dot(
        image, image.T, precision=lax.Precision.HIGHEST, preferred_element_type=jnp.float32
    )
    gram = lax.psum(partial_gram, ("wide", "narrow"))
    factor = factorize(gram)
    inverse = invert_upper(factor)
    scale = jnp.sqrt(jnp.float32(cells * lax.axis_size(("wide", "narrow"))))
    embedding = scale * jnp.dot(
        inverse.T, image, precision=lax.Precision.HIGHEST, preferred_element_type=jnp.float32
    )
    return (embedding, factor / scale)


def solution(mesh):
    in_specs = (
        P(None, ("wide", "narrow")),
        P(("wide", "narrow")),
        P(None, ("wide", "narrow")),
        P(None, ("wide", "narrow")),
    )
    out_specs = (P(None, ("wide", "narrow")), P())
    return jax.shard_map(body, mesh=mesh, in_specs=in_specs, out_specs=out_specs, check_vma=False)
```

profile of v0, /device:TPU:1, one launch (start us, length us, event | category | flops | bytes accessed | tf_op | source)
XLA Modules:
  0.0 643.5 jit_solution(140799619621341012)
XLA Ops:
  17.5 8.8 %collective-permute-done.3 = s32[1024]{0:T(1024)S(1)} collective-permute-done((s32[1024]{0:T(1024)S(1)}, s32[1024]{0:T(1024)S(1)}, u32[]{:S(2)}, u32[]{:S(2)}) %collective-permute-start.3) | collective-permute-done | bytes 4128 | tf_op jit(solution)/shard_map/ppermute | solution.py:12
  35.6 291.5 %while.48 = (s32[]{:T(128)}, f32[64,4096]{1,0:T(8,128)S(1)}, f32[4096]{0:T(1024)S(1)}, s32[10,8,512]{2,1,0:T(8,128)}, bf16[64,6144]{1,0:T(8,128)(2,1)S(1)}, /*in...) while((s32[]{:T(128)}, f32[64,4096]{1,0:T(8,128)S(1)}, ...), condition=%wide.region_2.4_spmd.clone.clone, body=%wide.region_0.3_spmd.clone.clone.sunk | while | flops 797529088 | bytes 23998728 | solution.py:98
  36.7 15.6 %fusion.86 = bf16[512,6144]{1,0:T(8,128)(2,1)} fusion(s32[512]{0:T(512)S(1)} %bitcast.95, s32[512]{0:T(512)S(1)} %bitcast.96, s32[512]{0:T(512)S(1)} %bitcast.97, s32[512]{0:T(512)S(1)} %bitcast.98, s32[512]{0:T(512)S(1)} %bitcast.99, s32[512]{0:T(512)S(1)} %bitcast.100, s32[512]{0:T(512)S(1)} %bitcast.101, s32[512]{0:T(512)S(1)} %bitcast.94), kind=kLoop, calls=%fused_computation.37.clone.1 | loop fusion | flops 100663296 | bytes 6307840 | tf_op jit(solution)/shard_map/while/body/eval_jaxpr/add | solution.py:77
  53.1 7.8 %convolution_add_fusion.2 = f32[64,4096]{1,0:T(8,128)S(1)} fusion(bf16[512,6144]{1,0:T(8,128)(2,1)} %fusion.86, bf16[64,6144]{1,0:T(8,128)(2,1)S(1)} %get-tuple-element.522, f32[64,4096]{1,0:T(8,128)S(1)} %get-tuple-element.505, pred[]{:T(512)S(6)} %compare.10, f32[512]{0:T(512)S(1)} %get-tuple-element.481), kind=kOutput, calls=%fused_computation.44.clone.1 | convolution fusion | flops 671678464 | bytes 13371393 | tf_op jit(solution)/shard_map/while/body/eval_jaxpr/dot_general | solution.py:85
  65.8 15.6 %fusion.86 = bf16[512,6144]{1,0:T(8,128)(2,1)} fusion(s32[512]{0:T(512)S(1)} %bitcast.95, s32[512]{0:T(512)S(1)} %bitcast.96, s32[512]{0:T(512)S(1)} %bitcast.97, s32[512]{0:T(512)S(1)} %bitcast.98, s32[512]{0:T(512)S(1)} %bitcast.99, s32[512]{0:T(512)S(1)} %bitcast.100, s32[512]{0:T(512)S(1)} %bitcast.101, s32[512]{0:T(512)S(1)} %bitcast.94), kind=kLoop, calls=%fused_computation.37.clone.1 | loop fusion | flops 100663296 | bytes 6307840 | tf_op jit(solution)/shard_map/while/body/eval_jaxpr/add | solution.py:77
  82.2 7.8 %convolution_add_fusion.2 = f32[64,4096]{1,0:T(8,128)S(1)} fusion(bf16[512,6144]{1,0:T(8,128)(2,1)} %fusion.86, bf16[64,6144]{1,0:T(8,128)(2,1)S(1)} %get-tuple-element.522, f32[64,4096]{1,0:T(8,128)S(1)} %get-tuple-element.505, pred[]{:T(512)S(6)} %compare.10, f32[512]{0:T(512)S(1)} %get-tuple-element.481), kind=kOutput, calls=%fused_computation.44.clone.1 | convolution fusion | flops 671678464 | bytes 13371393 | tf_op jit(solution)/shard_map/while/body/eval_jaxpr/dot_general | solution.py:85
  94.9 15.6 %fusion.86 = bf16[512,6144]{1,0:T(8,128)(2,1)} fusion(s32[512]{0:T(512)S(1)} %bitcast.95, s32[512]{0:T(512)S(1)} %bitcast.96, s32[512]{0:T(512)S(1)} %bitcast.97, s32[512]{0:T(512)S(1)} %bitcast.98, s32[512]{0:T(512)S(1)} %bitcast.99, s32[512]{0:T(512)S(1)} %bitcast.100, s32[512]{0:T(512)S(1)} %bitcast.101, s32[512]{0:T(512)S(1)} %bitcast.94), kind=kLoop, calls=%fused_computation.37.clone.1 | loop fusion | flops 100663296 | bytes 6307840 | tf_op jit(solution)/shard_map/while/body/eval_jaxpr/add | solution.py:77
  111.3 7.8 %convolution_add_fusion.2 = f32[64,4096]{1,0:T(8,128)S(1)} fusion(bf16[512,6144]{1,0:T(8,128)(2,1)} %fusion.86, bf16[64,6144]{1,0:T(8,128)(2,1)S(1)} %get-tuple-element.522, f32[64,4096]{1,0:T(8,128)S(1)} %get-tuple-element.505, pred[]{:T(512)S(6)} %compare.10, f32[512]{0:T(512)S(1)} %get-tuple-element.481), kind=kOutput, calls=%fused_computation.44.clone.1 | convolution fusion | flops 671678464 | bytes 13371393 | tf_op jit(solution)/shard_map/while/body/eval_jaxpr/dot_general | solution.py:85
  124.1 15.6 %fusion.86 = bf16[512,6144]{1,0:T(8,128)(2,1)} fusion(s32[512]{0:T(512)S(1)} %bitcast.95, s32[512]{0:T(512)S(1)} %bitcast.96, s32[512]{0:T(512)S(1)} %bitcast.97, s32[512]{0:T(512)S(1)} %bitcast.98, s32[512]{0:T(512)S(1)} %bitcast.99, s32[512]{0:T(512)S(1)} %bitcast.100, s32[512]{0:T(512)S(1)} %bitcast.101, s32[512]{0:T(512)S(1)} %bitcast.94), kind=kLoop, calls=%fused_computation.37.clone.1 | loop fusion | flops 100663296 | bytes 6307840 | tf_op jit(solution)/shard_map/while/body/eval_jaxpr/add | solution.py:77
  140.4 7.8 %convolution_add_fusion.2 = f32[64,4096]{1,0:T(8,128)S(1)} fusion(bf16[512,6144]{1,0:T(8,128)(2,1)} %fusion.86, bf16[64,6144]{1,0:T(8,128)(2,1)S(1)} %get-tuple-element.522, f32[64,4096]{1,0:T(8,128)S(1)} %get-tuple-element.505, pred[]{:T(512)S(6)} %compare.10, f32[512]{0:T(512)S(1)} %get-tuple-element.481), kind=kOutput, calls=%fused_computation.44.clone.1 | convolution fusion | flops 671678464 | bytes 13371393 | tf_op jit(solution)/shard_map/while/body/eval_jaxpr/dot_general | solution.py:85
  153.4 15.6 %fusion.86 = bf16[512,6144]{1,0:T(8,128)(2,1)} fusion(s32[512]{0:T(512)S(1)} %bitcast.95, s32[512]{0:T(512)S(1)} %bitcast.96, s32[512]{0:T(512)S(1)} %bitcast.97, s32[512]{0:T(512)S(1)} %bitcast.98, s32[512]{0:T(512)S(1)} %bitcast.99, s32[512]{0:T(512)S(1)} %bitcast.100, s32[512]{0:T(512)S(1)} %bitcast.101, s32[512]{0:T(512)S(1)} %bitcast.94), kind=kLoop, calls=%fused_computation.37.clone.1 | loop fusion | flops 100663296 | bytes 6307840 | tf_op jit(solution)/shard_map/while/body/eval_jaxpr/add | solution.py:77
  169.8 7.8 %convolution_add_fusion.2 = f32[64,4096]{1,0:T(8,128)S(1)} fusion(bf16[512,6144]{1,0:T(8,128)(2,1)} %fusion.86, bf16[64,6144]{1,0:T(8,128)(2,1)S(1)} %get-tuple-element.522, f32[64,4096]{1,0:T(8,128)S(1)} %get-tuple-element.505, pred[]{:T(512)S(6)} %compare.10, f32[512]{0:T(512)S(1)} %get-tuple-element.481), kind=kOutput, calls=%fused_computation.44.clone.1 | convolution fusion | flops 671678464 | bytes 13371393 | tf_op jit(solution)/shard_map/while/body/eval_jaxpr/dot_general | solution.py:85
  182.5 15.6 %fusion.86 = bf16[512,6144]{1,0:T(8,128)(2,1)} fusion(s32[512]{0:T(512)S(1)} %bitcast.95, s32[512]{0:T(512)S(1)} %bitcast.96, s32[512]{0:T(512)S(1)} %bitcast.97, s32[512]{0:T(512)S(1)} %bitcast.98, s32[512]{0:T(512)S(1)} %bitcast.99, s32[512]{0:T(512)S(1)} %bitcast.100, s32[512]{0:T(512)S(1)} %bitcast.101, s32[512]{0:T(512)S(1)} %bitcast.94), kind=kLoop, calls=%fused_computation.37.clone.1 | loop fusion | flops 100663296 | bytes 6307840 | tf_op jit(solution)/shard_map/while/body/eval_jaxpr/add | solution.py:77
  198.9 7.8 %convolution_add_fusion.2 = f32[64,4096]{1,0:T(8,128)S(1)} fusion(bf16[512,6144]{1,0:T(8,128)(2,1)} %fusion.86, bf16[64,6144]{1,0:T(8,128)(2,1)S(1)} %get-tuple-element.522, f32[64,4096]{1,0:T(8,128)S(1)} %get-tuple-element.505, pred[]{:T(512)S(6)} %compare.10, f32[512]{0:T(512)S(1)} %get-tuple-element.481), kind=kOutput, calls=%fused_computation.44.clone.1 | convolution fusion | flops 671678464 | bytes 13371393 | tf_op jit(solution)/shard_map/while/body/eval_jaxpr/dot_general | solution.py:85
  211.7 15.6 %fusion.86 = bf16[512,6144]{1,0:T(8,128)(2,1)} fusion(s32[512]{0:T(512)S(1)} %bitcast.95, s32[512]{0:T(512)S(1)} %bitcast.96, s32[512]{0:T(512)S(1)} %bitcast.97, s32[512]{0:T(512)S(1)} %bitcast.98, s32[512]{0:T(512)S(1)} %bitcast.99, s32[512]{0:T(512)S(1)} %bitcast.100, s32[512]{0:T(512)S(1)} %bitcast.101, s32[512]{0:T(512)S(1)} %bitcast.94), kind=kLoop, calls=%fused_computation.37.clone.1 | loop fusion | flops 100663296 | bytes 6307840 | tf_op jit(solution)/shard_map/while/body/eval_jaxpr/add | solution.py:77
  228.0 7.8 %convolution_add_fusion.2 = f32[64,4096]{1,0:T(8,128)S(1)} fusion(bf16[512,6144]{1,0:T(8,128)(2,1)} %fusion.86, bf16[64,6144]{1,0:T(8,128)(2,1)S(1)} %get-tuple-element.522, f32[64,4096]{1,0:T(8,128)S(1)} %get-tuple-element.505, pred[]{:T(512)S(6)} %compare.10, f32[512]{0:T(512)S(1)} %get-tuple-element.481), kind=kOutput, calls=%fused_computation.44.clone.1 | convolution fusion | flops 671678464 | bytes 13371393 | tf_op jit(solution)/shard_map/while/body/eval_jaxpr/dot_general | solution.py:85
  240.8 15.6 %fusion.86 = bf16[512,6144]{1,0:T(8,128)(2,1)} fusion(s32[512]{0:T(512)S(1)} %bitcast.95, s32[512]{0:T(512)S(1)} %bitcast.96, s32[512]{0:T(512)S(1)} %bitcast.97, s32[512]{0:T(512)S(1)} %bitcast.98, s32[512]{0:T(512)S(1)} %bitcast.99, s32[512]{0:T(512)S(1)} %bitcast.100, s32[512]{0:T(512)S(1)} %bitcast.101, s32[512]{0:T(512)S(1)} %bitcast.94), kind=kLoop, calls=%fused_computation.37.clone.1 | loop fusion | flops 100663296 | bytes 6307840 | tf_op jit(solution)/shard_map/while/body/eval_jaxpr/add | solution.py:77
  257.2 7.8 %convolution_add_fusion.2 = f32[64,4096]{1,0:T(8,128)S(1)} fusion(bf16[512,6144]{1,0:T(8,128)(2,1)} %fusion.86, bf16[64,6144]{1,0:T(8,128)(2,1)S(1)} %get-tuple-element.522, f32[64,4096]{1,0:T(8,128)S(1)} %get-tuple-element.505, pred[]{:T(512)S(6)} %compare.10, f32[512]{0:T(512)S(1)} %get-tuple-element.481), kind=kOutput, calls=%fused_computation.44.clone.1 | convolution fusion | flops 671678464 | bytes 13371393 | tf_op jit(solution)/shard_map/while/body/eval_jaxpr/dot_general | solution.py:85
  269.9 15.6 %fusion.86 = bf16[512,6144]{1,0:T(8,128)(2,1)} fusion(s32[512]{0:T(512)S(1)} %bitcast.95, s32[512]{0:T(512)S(1)} %bitcast.96, s32[512]{0:T(512)S(1)} %bitcast.97, s32[512]{0:T(512)S(1)} %bitcast.98, s32[512]{0:T(512)S(1)} %bitcast.99, s32[512]{0:T(512)S(1)} %bitcast.100, s32[512]{0:T(512)S(1)} %bitcast.101, s32[512]{0:T(512)S(1)} %bitcast.94), kind=kLoop, calls=%fused_computation.37.clone.1 | loop fusion | flops 100663296 | bytes 6307840 | tf_op jit(solution)/shard_map/while/body/eval_jaxpr/add | solution.py:77
  299.0 15.6 %fusion.86 = bf16[512,6144]{1,0:T(8,128)(2,1)} fusion(s32[512]{0:T(512)S(1)} %bitcast.95, s32[512]{0:T(512)S(1)} %bitcast.96, s32[512]{0:T(512)S(1)} %bitcast.97, s32[512]{0:T(512)S(1)} %bitcast.98, s32[512]{0:T(512)S(1)} %bitcast.99, s32[512]{0:T(512)S(1)} %bitcast.100, s32[512]{0:T(512)S(1)} %bitcast.101, s32[512]{0:T(512)S(1)} %bitcast.94), kind=kLoop, calls=%fused_computation.37.clone.1 | loop fusion | flops 100663296 | bytes 6307840 | tf_op jit(solution)/shard_map/while/body/eval_jaxpr/add | solution.py:77
  315.4 7.8 %convolution_add_fusion.2 = f32[64,4096]{1,0:T(8,128)S(1)} fusion(bf16[512,6144]{1,0:T(8,128)(2,1)} %fusion.86, bf16[64,6144]{1,0:T(8,128)(2,1)S(1)} %get-tuple-element.522, f32[64,4096]{1,0:T(8,128)S(1)} %get-tuple-element.505, pred[]{:T(512)S(6)} %compare.10, f32[512]{0:T(512)S(1)} %get-tuple-element.481), kind=kOutput, calls=%fused_computation.44.clone.1 | convolution fusion | flops 671678464 | bytes 13371393 | tf_op jit(solution)/shard_map/while/body/eval_jaxpr/dot_general | solution.py:85
  328.2 109.2 %psum.7 = f32[64,64]{1,0:T(8,128)S(1)} all-reduce(f32[64,64]{1,0:T(8,128)S(1)} %fusion.45), channel_id=1, replica_groups=mesh['wide'=32,'narrow'=16] {'wide','narrow'}, use_global_device_ids=true, to_apply=%region_3.5 | all-reduce | flops 4096 | bytes 32768 | tf_op jit(solution)/shard_map/psum | solution.py:103
  437.4 100.5 %while.49 = (s32[]{:T(128)}, f32[64,64]{1,0:T(8,128)S(1)}, f32[64,64]{1,0:T(8,128)S(1)}, s32[]{:T(128)}, s32[]{:T(128)}) while((s32[]{:T(128)}, f32[64,64]{1,0:T(8,128)S(1)}, f32[64,64]{1,0:T(8,128)S(1)}, s32[]{:T(128)}, s32[]{:T(128)}) %tuple.120), condition=%wide.region_6.8_spmd.clone.clone, body=%wide.region_4.7_spmd.clone.clone.sunk | while | flops 70210 | bytes 83555 | solution.py:32
  538.6 102.9 %while.47 = (s32[]{:T(128)}, f32[64,64]{1,0:T(8,128)S(1)}, f32[64,64]{1,0:T(8,128)S(1)}, s32[]{:T(128)}, s32[]{:T(128)}, /*index=5*/s32[]{:T(128)}) while((s32[]{:T(128)}, f32[64,64]{1,0:T(8,128)S(1)}, f32[64,64]{1,0:T(8,128)S(1)}, s32[]{:T(128)}, s32[]{:T(128)}, /*index=5*/s32[]{:T(128)}) %tuple.126), condition=%wide.region_9.11_spmd.clone, body=%wide.region_7.10_spmd.clone.sunk | while | flops 115331 | bytes 67184 | solution.py:53
  (597 shorter events, 253.2 us)
Async XLA Ops:
  0.6 34.9 %copy-start = (bf16[64,4096]{1,0:T(8,128)(2,1)S(1)}, bf16[64,4096]{1,0:T(8,128)(2,1)}, u32[]{:S(2)}) copy-start(bf16[64,4096]{1,0:T(8,128)(2,1)} %param.12) | copy-start | bytes 1572868
  1.4 16.1 %collective-permute-start.1 = (s32[1024]{0:T(1024)S(1)}, s32[1024]{0:T(1024)S(1)}, u32[]{:S(2)}, u32[]{:S(2)}) collective-permute-start(s32[1024]{0:T(1024)S(1)} %bitcast.105), channel_id=1, source_target_pairs={{0,1},{1,2},{2,3},{3,4},{4,5},{5,6},{6,7},{7,8},{8,9},{9,10},{10,1... | collective-permute-start | bytes 12296 | tf_op jit(solution)/shard_map/ppermute | solution.py:12
  5.4 21.0 %collective-permute-start = (bf16[64,4096]{1,0:T(8,128)(2,1)}, bf16[64,4096]{1,0:T(8,128)(2,1)S(1)}, u32[]{:S(2)}, u32[]{:S(2)}) collective-permute-start(bf16[64,4096]{1,0:T(8,128)(2,1)} %param.12), channel_id=1, source_target_pairs={{0,1},{1,2},{2,3},{3,4},{4,5},{5,6},{6,7},{7,8},{8,9},{9,10},{10,1... | collective-permute-start | bytes 1572872 | tf_op jit(solution)/shard_map/ppermute | solution.py:12
  8.5 21.9 %collective-permute-start.2 = (bf16[64,4096]{1,0:T(8,128)(2,1)}, bf16[64,4096]{1,0:T(8,128)(2,1)}, u32[]{:S(2)}, u32[]{:S(2)}) collective-permute-start(bf16[64,4096]{1,0:T(8,128)(2,1)} %param.12), channel_id=1, source_target_pairs={{0,511},{1,0},{2,1},{3,2},{4,3},{5,4},{6,5},{7,6},{8,7},{9,8},{10,... | collective-permute-start | bytes 1572872 | tf_op jit(solution)/shard_map/ppermute | solution.py:12
  14.3 12.1 %collective-permute-start.3 = (s32[1024]{0:T(1024)S(1)}, s32[1024]{0:T(1024)S(1)}, u32[]{:S(2)}, u32[]{:S(2)}) collective-permute-start(s32[1024]{0:T(1024)S(1)} %bitcast.104), channel_id=1, source_target_pairs={{0,511},{1,0},{2,1},{3,2},{4,3},{5,4},{6,5},{7,6},{8,7},{9,8},{10,... | collective-permute-start | bytes 12296 | tf_op jit(solution)/shard_map/ppermute | solution.py:12
  35.6 291.5 %copy-start.1 = (f32[4096]{0:T(1024)S(1)}, f32[4096]{0:T(1024)}, u32[]{:S(2)}) copy-start(f32[4096]{0:T(1024)} %param.13) | copy-start | bytes 49156
where the time goes:
time: 647 us; the launch traced here: 644 us
  matrix products  268 us (41%)
  other arithmetic  176 us (27%)
  blocking collectives  109 us (17%)
  loops' own time  45.1 us (7%)
  local copies, waits for them, and re-layouts  20.1 us (3%)
  starting transfers between devices  16 us (2%)
  waiting for transfers between devices  8.85 us (1%)
    add x10, other arithmetic, one_block(): incidence + (pin_block[slot][:, None] == column).astype(jnp.bfloat16)  156 us
    psum x1, blocking collectives, body(): gram = lax.psum(partial_gram, ('wide', 'narrow'))  109 us
    dot_general x10, matrix products, one_block(): jnp.dot(scaled, local, preferred_element_type=jnp.float32)  77.7 us
    dot_general x64, matrix products, one_column(): jnp.dot(rest, unit, precision=lax.Precision.HIGHEST, preferred_element_ty...  50.3 us
    dot_general x64, matrix products, one_row(): jnp.dot(unit, factor, precision=lax.Precision.HIGHEST, preferred_element_...  49.7 us
    dot_general x64, matrix products, one_row(): jnp.dot(row, solved, precision=lax.Precision.HIGHEST, preferred_element_t...  47.6 us
    another operation x1, loops' own time, factorize(): _, lower = lax.fori_loop(0, width, one_column, start)  44.4 us
    dot_general x10, matrix products, one_block(): jnp.dot((weight * size)[None, :], local.astype(jnp.float32), precision=la...  39.2 us
  transfers between devices with their start and end apart: 4, of which 1 were waited for; matrix products, arithmetic and copies ran while one was open for 1% of the time, Pallas kernels for 0%

commit v1 on v0

v1 whole, which is shorter than its diff:
```python
import functools

import jax
import jax.numpy as jnp
from jax import lax
from jax.experimental import pallas as pl
from jax.experimental.pallas import tpu as pltpu
from jax.sharding import PartitionSpec as P

BOTH = ("wide", "narrow")
HIGHEST = lax.Precision.HIGHEST
BLOCK = 512
CHUNK = 1024
VMEM_LIMIT = 60 << 20


def shifted(value, steps):
    count = lax.axis_size(BOTH)
    pairs = [(source, (source + steps) % count) for source in range(count)]
    return lax.ppermute(value, BOTH, pairs)


def image_kernel(
    pins_ref, vectors_ref, prev_ref, next_ref, anchors_ref,
    image_ref, gram_ref,
    extended, contrib, inc_even, inc_odd, pin_tile, count_tile, t_even, t_odd, sums,
):
    width, cells = vectors_ref.shape
    bound = prev_ref.shape[1]
    total = cells + 2 * bound
    slots, nets = pins_ref.shape
    incs = (inc_even, inc_odd)
    scaled = (t_even, t_odd)
    blocks = nets // BLOCK

    extended[:, :cells] = vectors_ref[...]
    extended[:, cells : cells + bound] = prev_ref[...]
    extended[:, cells + bound :] = next_ref[...]
    contrib[...] = jnp.zeros_like(contrib)

    def prepare(block):
        pins = pins_ref[:, block * BLOCK : (block + 1) * BLOCK]
        count = jnp.zeros((slots, BLOCK), jnp.int32)
        for slot in range(slots):
            count = count + (pins == pins[slot : slot + 1, :]).astype(jnp.int32)
        for slot in range(slots):
            row = pins[slot : slot + 1, :]
            pin_tile[slot] = jnp.broadcast_to(row, (16, BLOCK)).astype(jnp.int16)
            times = count[slot : slot + 1, :].astype(jnp.float32)
            count_tile[slot] = jnp.broadcast_to(times, (16, BLOCK)).astype(jnp.bfloat16)
        sums[...] = jnp.zeros_like(sums)

    def build(chunk):
        start = (chunk * CHUNK).astype(jnp.int16)
        local = [pin_tile[slot] - start for slot in range(slots)]
        lane = lax.broadcasted_iota(jnp.int32, (16, BLOCK), 0).astype(jnp.int16)
        rows = []
        for row in range(CHUNK // 16):
            place = lane + jnp.int16(16 * row)
            value = jnp.zeros((16, BLOCK), jnp.bfloat16)
            for slot in range(slots):
                value = jnp.where(local[slot] == place, count_tile[slot], value)
            rows.append(value)
        return jnp.concatenate(rows, axis=0)

    def finish(block):
        pins = pins_ref[:, block * BLOCK : (block + 1) * BLOCK]
        size = jnp.sum((pins >= 0).astype(jnp.float32), axis=0, keepdims=True)
        weight = 1.0 / (size - 1.0)
        target = scaled[block % 2]
        target[:width, :] = (sums[...] * weight).astype(jnp.bfloat16)
        degree = weight * size
        first = degree.astype(jnp.bfloat16).astype(jnp.float32)
        second = (degree - first).astype(jnp.bfloat16).astype(jnp.float32)
        third = degree - first - second
        row = lax.broadcasted_iota(jnp.int32, (16, BLOCK), 0)
        parts = jnp.where(row == 0, first, jnp.where(row == 1, second, jnp.where(row == 2, third, 0.0)))
        target[width:, :] = parts.astype(jnp.bfloat16)

    def step(block, spread, chunk):
        base = pl.multiple_of(chunk * CHUNK, CHUNK)
        if spread:
            added = lax.dot_general(
                scaled[1 - block % 2][...],
                incs[1 - block % 2][pl.ds(base, CHUNK), :],
                (((1,), (1,)), ((), ())),
                preferred_element_type=jnp.float32,
            )
        if block < blocks:
            tile = build(chunk)
            incs[block % 2][pl.ds(base, CHUNK), :] = tile
            sums[...] += jnp.dot(
                extended[:, pl.ds(base, CHUNK)], tile, preferred_element_type=jnp.float32
            )
        if spread:
            contrib[:, pl.ds(base, CHUNK)] += added

    for block in range(blocks + 1):
        if block < blocks:
            prepare(block)

        def near(chunk, carry):
            step(block, block > 0, chunk)
            return carry

        def far(chunk, carry):
            step(block, False, chunk)
            return carry

        lax.fori_loop(0, cells // CHUNK, near, 0)
        if block < blocks:
            lax.fori_loop(cells // CHUNK, total // CHUNK, far, 0)
            finish(block)

    degree = contrib[width : width + 1, :] + contrib[width + 1 : width + 2, :] + contrib[width + 2 : width + 3, :]
    image = (degree + anchors_ref[...]) * vectors_ref[...].astype(jnp.float32) - contrib[:width, :]
    image_ref[...] = image
    gram_ref[...] = lax.dot_general(
        image, image, (((1,), (1,)), ((), ())), precision=HIGHEST, preferred_element_type=jnp.float32
    )


def image_and_gram(pins, vectors, from_prev, from_next, anchors):
    width, cells = vectors.shape
    total = cells + 2 * from_prev.shape[1]
    slots = pins.shape[0]
    whole = pl.BlockSpec(memory_space=pltpu.VMEM)
    return pl.pallas_call(
        image_kernel,
        out_shape=(
            jax.ShapeDtypeStruct((width, cells), jnp.float32),
            jax.ShapeDtypeStruct((width, width), jnp.float32),
        ),
        in_specs=[whole] * 5,
        out_specs=(whole, whole),
        scratch_shapes=[
            pltpu.VMEM((width, total), jnp.bfloat16),
            pltpu.VMEM((width + 16, cells), jnp.float32),
            pltpu.VMEM((total, BLOCK), jnp.bfloat16),
            pltpu.VMEM((total, BLOCK), jnp.bfloat16),
            pltpu.VMEM((slots, 16, BLOCK), jnp.int16),
            pltpu.VMEM((slots, 16, BLOCK), jnp.bfloat16),
            pltpu.VMEM((width + 16, BLOCK), jnp.bfloat16),
            pltpu.VMEM((width + 16, BLOCK), jnp.bfloat16),
            pltpu.VMEM((width, BLOCK), jnp.float32),
        ],
        compiler_params=pltpu.CompilerParams(vmem_limit_bytes=VMEM_LIMIT),
    )(pins, vectors, from_prev, from_next, anchors[None, :])


def factor_kernel(scale, gram_ref, image_ref, embedding_ref, factor_ref):
    width = gram_ref.shape[0]
    rows = lax.broadcasted_iota(jnp.int32, (width, 2 * width), 0)
    columns = lax.broadcasted_iota(jnp.int32, (width, 2 * width), 1)
    unit = (columns == rows + width).astype(jnp.float32)
    work = jnp.concatenate([gram_ref[...], jnp.zeros((width, width), jnp.float32)], axis=1) + unit
    pivots = []
    for index in range(width):
        base = index // 8 * 8
        part = work[base:]
        row = work[index : index + 1]
        pivot = work[index : index + 1, index : index + 1]
        pivots.append(pivot)
        column = jnp.where(rows[base:] > index, part[:, index : index + 1], 0.0)
        part = part - column * (row * (1.0 / pivot))
        work = jnp.concatenate([work[:base], part], axis=0) if base else part
    work = work / jnp.sqrt(jnp.concatenate(pivots, axis=0))
    upper = columns[:, :width] >= rows[:, :width]
    factor_ref[...] = jnp.where(upper, work[:, :width], 0.0) / scale
    embedding_ref[...] = jnp.dot(
        work[:, width:] * scale, image_ref[...], precision=HIGHEST, preferred_element_type=jnp.float32
    )


def factor_and_embed(gram, image, scale):
    whole = pl.BlockSpec(memory_space=pltpu.VMEM)
    return pl.pallas_call(
        functools.partial(factor_kernel, scale),
        out_shape=(
            jax.ShapeDtypeStruct(image.shape, jnp.float32),
            jax.ShapeDtypeStruct(gram.shape, jnp.float32),
        ),
        in_specs=[whole, whole],
        out_specs=(whole, whole),
        compiler_params=pltpu.CompilerParams(vmem_limit_bytes=VMEM_LIMIT),
    )(gram, image)


def body(vectors, anchors, pins, halo_rows):
    cells = vectors.shape[1]
    up = jnp.take(vectors, halo_rows[0], axis=1)
    down = jnp.take(vectors, halo_rows[1], axis=1)
    from_prev = shifted(up, 1)
    from_next = shifted(down, -1)
    image, gram = image_and_gram(pins, vectors, from_prev, from_next, anchors)
    gram = jnp.sum(lax.all_gather(gram, "narrow"), axis=0)
    gram = jnp.sum(lax.all_gather(gram, "wide"), axis=0)
    scale = float(cells * lax.axis_size(BOTH)) ** 0.5
    return factor_and_embed(gram, image, scale)


def solution(mesh):
    in_specs = (P(None, BOTH), P(BOTH), P(None, BOTH), P(None, BOTH))
    out_specs = (P(None, BOTH), P())
    return jax.shard_map(body, mesh=mesh, in_specs=in_specs, out_specs=out_specs, check_vma=False)
```

time: 647 us -> 155 us (0.24)
  matrix products: 268 us -> 0 us
  other arithmetic: 176 us -> 0.81 us
  Pallas kernels: 0 us -> 67.2 us
  loops' own time: 45.1 us -> 0 us
  blocking collectives: 109 us -> 64.6 us
  local copies, waits for them, and re-layouts: 20.1 us -> 9.62 us
  waiting for transfers between devices: 8.85 us -> 1.91 us
    dot_general x214 -> x0, matrix products: 268 us -> none  [the longest x10 77.7 us: one_block(): jnp.dot(scaled, local, preferred_element_type=jnp.float32)]
    add x149 -> x0, other arithmetic: 167 us -> none  [the longest x10 156 us: one_block(): incidence + (pin_block[slot][:, None] == column).astype(jnp.bfloat16)]
    psum x1 -> x0, blocking collectives: 109 us -> none  [body(): gram = lax.psum(partial_gram, ('wide', 'narrow'))]
    pallas_call x0 -> x2, Pallas kernels: none -> 67.2 us  [the longest x1 58.6 us: image_and_gram(): pl.pallas_call(image_kernel, out_shape=(jax.ShapeDtypeStruct((width, cell...]
    all_gather x0 -> x2, blocking collectives: none -> 64.6 us  [the longest x1 42.4 us: body(): gram = jnp.sum(lax.all_gather(gram, 'wide'), axis=0)]
    another operation x3 -> x0, loops' own time: 45.1 us -> none  [the longest x1 44.4 us: factorize(): _, lower = lax.fori_loop(0, width, one_column, start)]
    slice x11 -> x1, local copies, waits for them, and re-layouts: 11.3 us -> 0.78 us  [body(): down = jnp.take(vectors, halo_rows[1], axis=1)]
    ppermute x4 -> x2, waiting for transfers between devices: 8.85 us -> 1.91 us  [shifted(): return lax.ppermute(value, BOTH, pairs)]
  transfers between devices with their start and end apart: 4 -> 2, of which waited for: 1 -> 1; matrix products, arithmetic and copies ran while one was open for 1% -> 2% of each run, Pallas kernels for 0% -> 0%
where the time goes in v1:
time: 155 us
  Pallas kernels  67.2 us (43%)
  blocking collectives  64.6 us (42%)
  starting transfers between devices  10.1 us (7%)
  local copies, waits for them, and re-layouts  9.62 us (6%)
  waiting for transfers between devices  1.91 us (1%)
    pallas_call x1, Pallas kernels, image_and_gram(): pl.pallas_call(image_kernel, out_shape=(jax.ShapeDtypeStruct((width, cell...  58.6 us
    all_gather x1, blocking collectives, body(): gram = jnp.sum(lax.all_gather(gram, 'wide'), axis=0)  42.4 us
    all_gather x1, blocking collectives, body(): gram = jnp.sum(lax.all_gather(gram, 'narrow'), axis=0)  22.3 us
    ppermute x2, starting transfers between devices, shifted(): return lax.ppermute(value, BOTH, pairs)  10.1 us
    pallas_call x1, Pallas kernels, factor_and_embed(): pl.pallas_call(functools.partial(factor_kernel, scale), out_shape=(jax.Sh...  8.61 us
    gather x2, local copies, waits for them, and re-layouts, body(): down = jnp.take(vectors, halo_rows[1], axis=1)  3.34 us
    gather x2, local copies, waits for them, and re-layouts, body(): up = jnp.take(vectors, halo_rows[0], axis=1)  3.34 us
  transfers between devices with their start and end apart: 2, of which 1 were waited for; matrix products, arithmetic and copies ran while one was open for 2% of the time, Pallas kernels for 0%

profile of v1, /device:TPU:1, one launch (start us, length us, event | category | flops | bytes accessed | tf_op | source)
XLA Modules:
  0.0 155.0 jit_solution(127487601154804157)
XLA Ops:
  0.6 0.8 fusion.2
  1.4 1.5 copy.10
  3.0 3.2 %gather_fusion = bf16[1024,64]{1,0:T(8,128)(2,1)S(1)} fusion(bf16[64,4096]{0,1:T(8,128)(2,1)S(1)} %copy.10, s32[1024]{0:T(1024)S(1)} %fusion), kind=kCustom, calls=%fused_computation.clone | custom fusion | bytes 266240 | tf_op jit(solution)/shard_map/jit(_take)/gather | solution.py:191
  6.2 0.1 copy.11
  6.3 3.9 %collective-permute-start = (bf16[64,1024]{1,0:T(8,128)(2,1)S(1)}, bf16[64,1024]{1,0:T(8,128)(2,1)S(1)}, u32[]{:S(2)}, u32[]{:S(2)}) collective-permute-start(bf16[64,1024]{1,0:T(8,128)(2,1)S(1)} %select_bitcast_fusion.1), channel_id=1, source_target_pairs={{0,1},{1,2},{2,3},{3,4},{4,5},{5,6},{6,7},{7,8},{8,9},{9,10},{10,1... | collective-permute-start | bytes 393224 | tf_op jit(solution)/shard_map/ppermute | solution.py:20
  10.3 3.2 %gather_fusion.1 = bf16[1024,64]{1,0:T(8,128)(2,1)S(1)} fusion(bf16[64,4096]{0,1:T(8,128)(2,1)S(1)} %copy.10, s32[1024]{0:T(1024)S(1)} %fusion.1), kind=kCustom, calls=%fused_computation.1.clone | custom fusion | bytes 266240 | tf_op jit(solution)/shard_map/jit(_take)/gather | solution.py:192
  13.5 0.1 copy.13
  13.7 6.2 %collective-permute-start.1 = (bf16[64,1024]{1,0:T(8,128)(2,1)S(1)}, bf16[64,1024]{1,0:T(8,128)(2,1)S(1)}, u32[]{:S(2)}, u32[]{:S(2)}) collective-permute-start(bf16[64,1024]{1,0:T(8,128)(2,1)S(1)} %select_bitcast_fusion), channel_id=1, source_target_pairs={{0,511},{1,0},{2,1},{3,2},{4,3},{5,4},{6,5},{7,6},{8,7},{9,8},{10,... | collective-permute-start | bytes 393224 | tf_op jit(solution)/shard_map/ppermute | solution.py:20
  19.9 0.0 collective-permute-done.prev_ref
  19.9 0.0 copy-start
  19.9 1.9 %collective-permute-done.1.next_ref = bf16[64,1024]{1,0:T(8,128)(2,1)S(1)} collective-permute-done((bf16[64,1024]{1,0:T(8,128)(2,1)S(1)}, bf16[64,1024]{1,0:T(8,128)(2,1)S(1)}, u32[]{:S(2)}, u32[]{:S(2)}) %collective-permute-start.1) | collective-permute-done | bytes 131104 | tf_op jit(solution)/shard_map/ppermute | solution.py:20
  21.8 0.0 copy-start.1
  21.8 0.0 copy-done
  21.8 0.6 copy-done.1
  22.5 58.6 %shard_map.59 = (f32[64,4096]{1,0:T(8,128)}, f32[64,64]{1,0:T(8,128)}) custom-call(s32[8,5120]{1,0:T(8,128)} %pins_ref.1, bf16[64,4096]{1,0:T(8,128)(2,1)} %vectors_ref.1, bf16[64,1024]{1,0:T(8,128)(2,1)} %copy-done, bf16[64,1024]{1,0:T(8,128)(2,1)} %copy-done.1, f32[1,4096]{1,0:T(1,128)} %bitcast.15), custom_call_target="tpu_custom_call" | custom-call | tf_op jit(solution)/shard_map/pallas_call | solution.py:128
  81.0 22.3 %all-gather = f32[1024,64]{1,0:T(8,128)S(1)} all-gather(f32[64,64]{1,0:T(8,128)} %get-tuple-element.5), channel_id=2, replica_groups=mesh['wide'=32,'narrow'=16] {'narrow'}, dimensions={0}, use_global_device_ids=true | all-gather | bytes 278528 | tf_op jit(solution)/shard_map/all_gather | solution.py:196
  103.3 42.4 %all-gather.1 = f32[2048,64]{1,0:T(8,128)S(1)} all-gather(f32[64,64]{1,0:T(8,128)S(1)} %reduce_sum.18), channel_id=3, replica_groups=mesh['wide'=32,'narrow'=16] {'wide'}, dimensions={0}, use_global_device_ids=true | all-gather | bytes 540672 | tf_op jit(solution)/shard_map/all_gather | solution.py:197
  145.7 0.7 reduce_sum.19.gram_ref
  146.4 8.6 %shard_map.60 = (f32[64,4096]{1,0:T(8,128)}, f32[64,64]{1,0:T(8,128)}) custom-call(f32[64,64]{1,0:T(8,128)} %reduce_sum.19.gram_ref, f32[64,4096]{1,0:T(8,128)} %get-tuple-element.6.image_ref), custom_call_target="tpu_custom_call" | custom-call | tf_op jit(solution)/shard_map/pallas_call | solution.py:177
  (7 shorter events, 0.1 us)
Async XLA Ops:
  6.3 13.6 %collective-permute-start = (bf16[64,1024]{1,0:T(8,128)(2,1)S(1)}, bf16[64,1024]{1,0:T(8,128)(2,1)S(1)}, u32[]{:S(2)}, u32[]{:S(2)}) collective-permute-start(bf16[64,1024]{1,0:T(8,128)(2,1)S(1)} %select_bitcast_fusion.1), channel_id=1, source_target_pairs={{0,1},{1,2},{2,3},{3,4},{4,5},{5,6},{6,7},{7,8},{8,9},{9,10},{10,1... | collective-permute-start | bytes 393224 | tf_op jit(solution)/shard_map/ppermute | solution.py:20
  13.7 8.1 %collective-permute-start.1 = (bf16[64,1024]{1,0:T(8,128)(2,1)S(1)}, bf16[64,1024]{1,0:T(8,128)(2,1)S(1)}, u32[]{:S(2)}, u32[]{:S(2)}) collective-permute-start(bf16[64,1024]{1,0:T(8,128)(2,1)S(1)} %select_bitcast_fusion), channel_id=1, source_target_pairs={{0,511},{1,0},{2,1},{3,2},{4,3},{5,4},{6,5},{7,6},{8,7},{9,8},{10,... | collective-permute-start | bytes 393224 | tf_op jit(solution)/shard_map/ppermute | solution.py:20
  19.9 1.9 %copy-start = (bf16[64,1024]{1,0:T(8,128)(2,1)}, bf16[64,1024]{1,0:T(8,128)(2,1)S(1)}, u32[]{:S(2)}) copy-start(bf16[64,1024]{1,0:T(8,128)(2,1)S(1)} %collective-permute-done.prev_ref) | copy-start | bytes 393220
  21.8 0.7 copy-start.1

commit v2 on v1

v2 whole, which is shorter than its diff:
```python
import functools

import jax
import jax.numpy as jnp
from jax import lax
from jax.experimental import pallas as pl
from jax.experimental.pallas import tpu as pltpu
from jax.sharding import PartitionSpec as P

BOTH = ("wide", "narrow")
HIGHEST = lax.Precision.HIGHEST
BLOCK = 512
CHUNK = 256
FIELDS = 4
PICK = 512
SPAN = 4096
AHEAD = 2
VMEM_LIMIT = 60 << 20


def shifted(value, steps):
    count = lax.axis_size(BOTH)
    pairs = [(source, (source + steps) % count) for source in range(count)]
    return lax.ppermute(value, BOTH, pairs)


def pick_kernel(rows_ref, vectors_ref, up_ref, down_ref):
    width, cells = vectors_ref.shape
    count = rows_ref.shape[1]
    lane = lax.broadcasted_iota(jnp.int32, (16, PICK), 0).astype(jnp.int16)
    for direction, picked_ref in enumerate((up_ref, down_ref)):
        for part in range(count // PICK):
            columns = slice(part * PICK, (part + 1) * PICK)
            wanted = rows_ref[direction : direction + 1, columns]
            wanted = jnp.broadcast_to(wanted, (16, PICK)).astype(jnp.int16)

            def step(chunk, total):
                base = pl.multiple_of(chunk * SPAN, SPAN)
                local = wanted - (chunk * SPAN).astype(jnp.int16)
                tile = [
                    jnp.where(local == lane + jnp.int16(16 * row), jnp.bfloat16(1), jnp.bfloat16(0))
                    for row in range(SPAN // 16)
                ]
                return total + jnp.dot(
                    vectors_ref[:, pl.ds(base, SPAN)],
                    jnp.concatenate(tile, axis=0),
                    preferred_element_type=jnp.float32,
                )

            total = lax.fori_loop(0, cells // SPAN, step, jnp.zeros((width, PICK), jnp.float32))
            picked_ref[:, columns] = total.astype(jnp.bfloat16)


def pick(halo_rows, vectors):
    whole = pl.BlockSpec(memory_space=pltpu.VMEM)
    width, cells = vectors.shape
    count = halo_rows.shape[1]
    picked = jax.ShapeDtypeStruct((width, count), jnp.bfloat16)
    return pl.pallas_call(
        pick_kernel,
        out_shape=(picked, picked),
        in_specs=[whole, whole],
        out_specs=(whole, whole),
        cost_estimate=pl.CostEstimate(
            flops=4 * width * cells * count, bytes_accessed=2 * width * cells, transcendentals=0
        ),
        compiler_params=pltpu.CompilerParams(vmem_limit_bytes=VMEM_LIMIT),
    )(halo_rows, vectors)


def spread_pins(stride, pins, place_tile, value_tile):
    slots, block = pins.shape
    field = jnp.zeros(pins.shape, jnp.int32)
    for index in range(1, FIELDS):
        field = field + (pins >= index * stride).astype(jnp.int32)
    place = pins - field * stride
    value = jnp.where(field == 0, 1, jnp.where(field == 1, 16, jnp.where(field == 2, 256, 4096)))
    for slot in range(slots):
        place_tile[slot] = jnp.broadcast_to(place[slot : slot + 1, :], (16, block)).astype(jnp.int16)
        value_tile[slot] = jnp.broadcast_to(value[slot : slot + 1, :], (16, block)).astype(jnp.int16)


def build_words(chunk, extent, place_tile, value_tile):
    slots, sublanes, block = place_tile.shape
    lane = lax.broadcasted_iota(jnp.int32, (sublanes, block), 0).astype(jnp.int16)
    local = [place_tile[slot] - (chunk * extent).astype(jnp.int16) for slot in range(slots)]
    rows = []
    for row in range(extent // sublanes):
        here = lane + jnp.int16(sublanes * row)
        word = jnp.zeros((sublanes, block), jnp.int16)
        for slot in range(slots):
            word = word + jnp.where(local[slot] == here, value_tile[slot], jnp.int16(0))
        rows.append(word)
    return jnp.concatenate(rows, axis=0)


def words_kernel(pins_ref, words_ref, place_tile, value_tile):
    stride = words_ref.shape[0]
    spread_pins(stride, pins_ref[...], place_tile, value_tile)

    def step(chunk, carry):
        words_ref[pl.ds(pl.multiple_of(chunk * 512, 512), 512), :] = build_words(
            chunk, 512, place_tile, value_tile
        )
        return carry

    lax.fori_loop(0, stride // 512, step, 0)


def count_words(pins, total):
    slots = pins.shape[0]
    nets = 2 * BLOCK * AHEAD
    stride = total // FIELDS
    return pl.pallas_call(
        words_kernel,
        grid=(nets // BLOCK,),
        out_shape=jax.ShapeDtypeStruct((stride, nets), jnp.int16),
        in_specs=[pl.BlockSpec((slots, BLOCK), lambda step: (0, step))],
        out_specs=pl.BlockSpec((stride, BLOCK), lambda step: (0, step)),
        scratch_shapes=[pltpu.VMEM((slots, 16, BLOCK), jnp.int16)] * 2,
        cost_estimate=pl.CostEstimate(
            flops=24 * stride * nets, bytes_accessed=2 * stride * nets, transcendentals=0
        ),
        compiler_params=pltpu.CompilerParams(vmem_limit_bytes=VMEM_LIMIT),
    )(pins)


def image_kernel(
    words_ref, pins_ref, vectors_ref, prev_ref, next_ref, anchors_ref,
    image_ref, gram_ref,
    extended, contrib, inc_even, inc_odd, t_even, t_odd, sums, place_tile, value_tile,
):
    width, cells = vectors_ref.shape
    bound = prev_ref.shape[1]
    stride = words_ref.shape[0]
    incs = (inc_even, inc_odd)
    scaled = (t_even, t_odd)
    turn = pl.program_id(0)

    def finish(half):
        pins = pins_ref[:, half * BLOCK : (half + 1) * BLOCK]
        size = jnp.sum((pins >= 0).astype(jnp.float32), axis=0, keepdims=True)
        weight = 1.0 / (size - 1.0)
        target = scaled[half]
        target[:width, :] = (sums[...] * weight).astype(jnp.bfloat16)
        degree = weight * size
        first = degree.astype(jnp.bfloat16).astype(jnp.float32)
        second = (degree - first).astype(jnp.bfloat16).astype(jnp.float32)
        third = degree - first - second
        row = lax.broadcasted_iota(jnp.int32, (16, BLOCK), 0)
        parts = jnp.where(row == 0, first, jnp.where(row == 1, second, jnp.where(row == 2, third, 0.0)))
        target[width:, :] = parts.astype(jnp.bfloat16)

    def step(half, unpack, spread, owned, ahead, chunk):
        base = pl.multiple_of(chunk * CHUNK, CHUNK)
        added = []
        if spread is not None:
            for field in range(owned):
                place = pl.multiple_of(field * stride + base, CHUNK)
                added.append(
                    lax.dot_general(
                        scaled[spread][...],
                        incs[spread][pl.ds(place, CHUNK), :],
                        (((1,), (1,)), ((), ())),
                        preferred_element_type=jnp.float32,
                    )
                )
        if unpack:
            if ahead:
                words = words_ref[pl.ds(base, CHUNK), half * BLOCK : (half + 1) * BLOCK]
            else:
                words = build_words(chunk, CHUNK, place_tile, value_tile)
            fresh = jnp.zeros(sums.shape, jnp.float32)
            for field in range(FIELDS):
                place = pl.multiple_of(field * stride + base, CHUNK)
                tile = lax.shift_right_logical(words, jnp.int16(4 * field)) & jnp.int16(15)
                tile = tile.astype(jnp.bfloat16)
                if field < owned:
                    incs[half][pl.ds(place, CHUNK), :] = tile
                fresh = fresh + jnp.dot(
                    extended[:, pl.ds(place, CHUNK)], tile, preferred_element_type=jnp.float32
                )
            sums[...] += fresh
        for field, term in enumerate(added):
            place = pl.multiple_of(field * stride + base, CHUNK)
            contrib[:, pl.ds(place, CHUNK)] += term

    def sweep(half, unpack, spread, ahead):
        if unpack and not ahead:
            spread_pins(stride, pins_ref[:, half * BLOCK : (half + 1) * BLOCK], place_tile, value_tile)
        if unpack:
            sums[...] = jnp.zeros_like(sums)
        many = -(-cells // stride)
        edge = (cells - (many - 1) * stride) // CHUNK

        def low(chunk, carry):
            step(half, unpack, spread, many, ahead, chunk)
            return carry

        def high(chunk, carry):
            step(half, unpack, spread, many - 1, ahead, chunk)
            return carry

        lax.fori_loop(0, edge, low, 0)
        lax.fori_loop(edge, stride // CHUNK, high, 0)
        if unpack:
            finish(half)

    @pl.when(turn == 0)
    def _():
        extended[:, :cells] = vectors_ref[...]
        extended[:, cells : cells + bound] = prev_ref[...]
        extended[:, cells + bound :] = next_ref[...]
        contrib[...] = jnp.zeros_like(contrib)
        sweep(0, True, None, AHEAD > 0)

    @pl.when((turn > 0) & (turn < AHEAD))
    def _():
        sweep(0, True, 1, True)

    @pl.when((turn > 0) & (turn >= AHEAD))
    def _():
        sweep(0, True, 1, False)

    @pl.when(turn < AHEAD)
    def _():
        sweep(1, True, 0, True)

    @pl.when(turn >= AHEAD)
    def _():
        sweep(1, True, 0, False)

    @pl.when(turn == pl.num_programs(0) - 1)
    def _():
        sweep(1, False, 1, True)
        degree = (
            contrib[width : width + 1, :] + contrib[width + 1 : width + 2, :] + contrib[width + 2 : width + 3, :]
        )
        image = (degree + anchors_ref[...]) * vectors_ref[...].astype(jnp.float32) - contrib[:width, :]
        image_ref[...] = image
        gram = lax.dot_general(
            image, image, (((1,), (1,)), ((), ())), precision=HIGHEST, preferred_element_type=jnp.float32
        )
        fold = width // 2
        packed = jnp.concatenate([gram[:fold], gram[fold:]], axis=1)
        for copy in range(gram_ref.shape[0]):
            gram_ref[copy] = packed


def image_and_gram(words, pins, vectors, from_prev, from_next, anchors, copies):
    width, cells = vectors.shape
    slots, nets = pins.shape
    stride = words.shape[0]
    whole = pl.BlockSpec(memory_space=pltpu.VMEM)
    return pl.pallas_call(
        image_kernel,
        grid=(nets // (2 * BLOCK),),
        out_shape=(
            jax.ShapeDtypeStruct((width, cells), jnp.float32),
            jax.ShapeDtypeStruct((copies, width // 2, 2 * width), jnp.float32),
        ),
        in_specs=[
            pl.BlockSpec((stride, 2 * BLOCK), lambda step: (0, jnp.minimum(step, AHEAD - 1))),
            pl.BlockSpec((slots, 2 * BLOCK), lambda step: (0, step)),
        ]
        + [whole] * 4,
        out_specs=(whole, whole),
        scratch_shapes=[
            pltpu.VMEM((width, stride * FIELDS), jnp.bfloat16),
            pltpu.VMEM((width + 16, cells), jnp.float32),
            pltpu.VMEM((cells, BLOCK), jnp.bfloat16),
            pltpu.VMEM((cells, BLOCK), jnp.bfloat16),
            pltpu.VMEM((width + 16, BLOCK), jnp.bfloat16),
            pltpu.VMEM((width + 16, BLOCK), jnp.bfloat16),
            pltpu.VMEM((width, BLOCK), jnp.float32),
            pltpu.VMEM((slots, 16, BLOCK), jnp.int16),
            pltpu.VMEM((slots, 16, BLOCK), jnp.int16),
        ],
        compiler_params=pltpu.CompilerParams(vmem_limit_bytes=VMEM_LIMIT),
    )(words, pins, vectors, from_prev, from_next, anchors[None, :])


def summed_gram(copies):
    groups = lax.axis_size("wide")
    pairs = [[2 * chip, 2 * chip + 1] for chip in range(groups // 2)]
    columns = [[2 * chip + core for chip in range(groups // 2)] for core in range(2)]
    plane = jnp.sum(lax.all_to_all(copies, "narrow", 0, 0), axis=0)
    plane = jnp.sum(lax.all_gather(plane, "wide", axis_index_groups=pairs), axis=0)
    half = plane.shape[0] // 2
    start = lax.rem(lax.axis_index("wide"), 2) * half
    share = lax.dynamic_slice_in_dim(plane, start, half, axis=0)
    share = jnp.broadcast_to(share[None], (groups // 2,) + share.shape)
    share = jnp.sum(lax.all_to_all(share, "wide", 0, 0, axis_index_groups=columns), axis=0)
    return lax.all_gather(share, "wide", axis_index_groups=pairs, tiled=True)


def factor_kernel(scale, gram_ref, image_ref, embedding_ref, factor_ref):
    width = gram_ref.shape[1] // 2
    gram = jnp.concatenate([gram_ref[:, :width], gram_ref[:, width:]], axis=0)
    rows = lax.broadcasted_iota(jnp.int32, (width, 2 * width), 0)
    columns = lax.broadcasted_iota(jnp.int32, (width, 2 * width), 1)
    unit = (columns == rows + width).astype(jnp.float32)
    work = jnp.concatenate([gram, jnp.zeros((width, width), jnp.float32)], axis=1) + unit
    pivots = []
    for index in range(width):
        base = index // 8 * 8
        part = work[base:]
        row = work[index : index + 1]
        pivot = work[index : index + 1, index : index + 1]
        pivots.append(pivot)
        column = jnp.where(rows[base:] > index, part[:, index : index + 1], 0.0)
        part = part - column * (row * (1.0 / pivot))
        work = jnp.concatenate([work[:base], part], axis=0) if base else part
    work = work / jnp.sqrt(jnp.concatenate(pivots, axis=0))
    upper = columns[:, :width] >= rows[:, :width]
    factor_ref[...] = jnp.where(upper, work[:, :width], 0.0) / scale
    embedding_ref[...] = jnp.dot(
        work[:, width:] * scale, image_ref[...], precision=HIGHEST, preferred_element_type=jnp.float32
    )


def factor_and_embed(gram, image, scale):
    whole = pl.BlockSpec(memory_space=pltpu.VMEM)
    return pl.pallas_call(
        functools.partial(factor_kernel, scale),
        out_shape=(
            jax.ShapeDtypeStruct(image.shape, jnp.float32),
            jax.ShapeDtypeStruct((image.shape[0],) * 2, jnp.float32),
        ),
        in_specs=[whole, whole],
        out_specs=(whole, whole),
        compiler_params=pltpu.CompilerParams(vmem_limit_bytes=VMEM_LIMIT),
    )(gram, image)


def body(vectors, anchors, pins, halo_rows):
    cells = vectors.shape[1]
    total = cells + halo_rows.size
    up, down = pick(halo_rows, vectors)
    from_prev = shifted(up, 1)
    from_next = shifted(down, -1)
    words = count_words(pins, total)
    copies = lax.axis_size("narrow")
    image, gram = image_and_gram(words, pins, vectors, from_prev, from_next, anchors, copies)
    gram = summed_gram(gram)
    scale = float(cells * lax.axis_size(BOTH)) ** 0.5
    return factor_and_embed(gram, image, scale)


def solution(mesh):
    in_specs = (P(None, BOTH), P(BOTH), P(None, BOTH), P(None, BOTH))
    out_specs = (P(None, BOTH), P())
    return jax.shard_map(body, mesh=mesh, in_specs=in_specs, out_specs=out_specs, check_vma=False)
```

time: 155 us -> 126 us (0.81)
  blocking collectives: 64.6 us -> 36 us
  local copies, waits for them, and re-layouts: 9.62 us -> 0.71 us
  waiting for transfers between devices: 1.91 us -> 7.54 us
  starting transfers between devices: 10.1 us -> 14.4 us
    all_gather x2, blocking collectives: 64.6 us -> 15.5 us  [the longest x1 10.7 us: summed_gram(): lax.all_gather(plane, 'wide', axis_index_groups=pairs)]
    all_to_all x0 -> x1, blocking collectives: none -> 20.4 us  [summed_gram(): lax.all_to_all(share, 'wide', 0, 0, axis_index_groups=columns)]
    all_to_all x0 -> x1, waiting for transfers between devices: none -> 7.53 us  [summed_gram(): plane = jnp.sum(lax.all_to_all(copies, 'narrow', 0, 0), axis=0)]
    gather x4 -> x0, local copies, waits for them, and re-layouts: 6.67 us -> none  [the longest x2 3.34 us: body(): down = jnp.take(vectors, halo_rows[1], axis=1)]
    all_to_all x0 -> x1, starting transfers between devices: none -> 4.24 us  [summed_gram(): plane = jnp.sum(lax.all_to_all(copies, 'narrow', 0, 0), axis=0)]
    ppermute x2, waiting for transfers between devices: 1.91 us -> 0.01 us  [shifted(): return lax.ppermute(value, BOTH, pairs)]
    pallas_call x1 -> x3, Pallas kernels: 58.6 us -> 57.1 us  [the longest x1 45.3 us: image_and_gram(): pl.pallas_call(image_kernel, grid=(nets // (2 * BLOCK),), out_shape=(jax....]
  transfers between devices with their start and end apart: 2 -> 3, of which waited for: 1 -> 1; matrix products, arithmetic and copies ran while one was open for 2% -> 0% of each run, Pallas kernels for 0% -> 6%
where the time goes in v2:
time: 126 us; the launch traced here: 125 us
  Pallas kernels  65.7 us (52%)
  blocking collectives  36 us (29%)
  starting transfers between devices  14.4 us (11%)
  waiting for transfers between devices  7.54 us (6%)
    pallas_call x1, Pallas kernels, image_and_gram(): pl.pallas_call(image_kernel, grid=(nets // (2 * BLOCK),), out_shape=(jax....  45.3 us
    all_to_all x1, blocking collectives, summed_gram(): lax.all_to_all(share, 'wide', 0, 0, axis_index_groups=columns)  20.4 us
    all_gather x1, blocking collectives, summed_gram(): lax.all_gather(plane, 'wide', axis_index_groups=pairs)  10.7 us
    ppermute x2, starting transfers between devices, shifted(): return lax.ppermute(value, BOTH, pairs)  10.1 us
    pallas_call x1, Pallas kernels, factor_and_embed(): pl.pallas_call(functools.partial(factor_kernel, scale), out_shape=(jax.Sh...  8.63 us
    all_to_all x1, waiting for transfers between devices, summed_gram(): plane = jnp.sum(lax.all_to_all(copies, 'narrow', 0, 0), axis=0)  7.53 us
    pallas_call x1, Pallas kernels, count_words(): pl.pallas_call(words_kernel, grid=(nets // BLOCK,), out_shape=jax.ShapeDt...  7.08 us
    all_gather x1, blocking collectives, summed_gram(): return lax.all_gather(share, 'wide', axis_index_groups=pairs, tiled=True)  4.86 us
  transfers between devices with their start and end apart: 3, of which 1 were waited for; matrix products, arithmetic and copies ran while one was open for 0% of the time, Pallas kernels for 6%

profile of v2, /device:TPU:1, one launch (start us, length us, event | category | flops | bytes accessed | tf_op | source)
XLA Modules:
  0.0 125.0 jit_solution(2975584569582044978)
XLA Ops:
  0.6 4.7 %shard_map.60 = (bf16[64,1024]{1,0:T(8,128)(2,1)}, bf16[64,1024]{1,0:T(8,128)(2,1)}) custom-call(s32[2,1024]{1,0:T(2,128)} %rows_ref.1, bf16[64,4096]{1,0:T(8,128)(2,1)} %vectors_ref.3), custom_call_target="tpu_custom_call" | custom-call | flops 1073741824 | bytes 524288 | tf_op jit(solution)/shard_map/pallas_call | solution.py:59
  5.4 3.9 %collective-permute-start = (bf16[64,1024]{1,0:T(8,128)(2,1)}, bf16[64,1024]{1,0:T(8,128)(2,1)S(1)}, u32[]{:S(2)}, u32[]{:S(2)}) collective-permute-start(bf16[64,1024]{1,0:T(8,128)(2,1)} %get-tuple-element.6), channel_id=1, source_target_pairs={{0,1},{1,2},{2,3},{3,4},{4,5},{5,6},{6,7},{7,8},{8,9},{9,10},{10,1... | collective-permute-start | bytes 393224 | tf_op jit(solution)/shard_map/ppermute | solution.py:24
  9.3 6.2 %collective-permute-start.1 = (bf16[64,1024]{1,0:T(8,128)(2,1)}, bf16[64,1024]{1,0:T(8,128)(2,1)S(1)}, u32[]{:S(2)}, u32[]{:S(2)}) collective-permute-start(bf16[64,1024]{1,0:T(8,128)(2,1)} %get-tuple-element.7), channel_id=1, source_target_pairs={{0,511},{1,0},{2,1},{3,2},{4,3},{5,4},{6,5},{7,6},{8,7},{9,8},{10,... | collective-permute-start | bytes 393224 | tf_op jit(solution)/shard_map/ppermute | solution.py:24
  15.5 7.1 %shard_map.59.words_ref = s16[1536,2048]{1,0:T(8,128)(2,1)} custom-call(s32[8,5120]{1,0:T(8,128)} %pins_ref.3), custom_call_target="tpu_custom_call" | custom-call | flops 75497472 | bytes 6291456 | tf_op jit(solution)/shard_map/pallas_call | solution.py:114
  22.6 0.0 collective-permute-done.prev_ref
  22.6 0.0 copy-start
  22.6 0.0 collective-permute-done.1.next_ref
  22.6 0.0 copy-start.1
  22.6 0.6 copy-done
  23.2 0.1 copy-done.1
  23.3 45.3 %shard_map.61 = (f32[64,4096]{1,0:T(8,128)}, f32[16,32,128]{2,1,0:T(8,128)}) custom-call(s16[1536,2048]{1,0:T(8,128)(2,1)} %shard_map.59.words_ref, s32[8,5120]{1,0:T(8,128)} %pins_ref.3, bf16[64,4096]{1,0:T(8,128)(2,1)} %vectors_ref.3, bf16[64,1024]{1,0:T(8,128)(2,1)} %copy-done, bf16[64,1024]{1,0:T(8,128)(2,1)} %copy-done.1, f32[1,4096]{1,0:T(1,128)} %bitcast.3), custom_call_target="tpu_custom_call" | custom-call | tf_op jit(solution)/shard_map/pallas_call | solution.py:255
  68.5 4.2 %all-to-all-start = ((f32[16,32,128]{2,1,0:T(8,128)}), f32[16,32,128]{2,1,0:T(8,128)S(1)}, u32[]{:S(2)}, u32[]{:S(2)}) async-start(f32[16,32,128]{2,1,0:T(8,128)} %get-tuple-element.8), calls=%async_computation | async-start | bytes 524288 | tf_op jit(solution)/shard_map/all_to_all | solution.py:287
  72.8 7.5 %all-to-all-done = f32[16,32,128]{2,1,0:T(8,128)S(1)} async-done(((f32[16,32,128]{2,1,0:T(8,128)}), f32[16,32,128]{2,1,0:T(8,128)S(1)}, u32[]{:S(2)}, u32[]{:S(2)}) %all-to-all-start) | async-done | bytes 262176 | tf_op jit(solution)/shard_map/all_to_all | solution.py:287
  80.4 10.7 %all-gather = f32[64,128]{1,0:T(8,128)S(1)} all-gather(f32[32,128]{1,0:T(8,128)S(1)} %reduce_sum.27), channel_id=2, replica_groups={{0,16},{32,48},{64,80},{96,112},{128,144},{160,176},{192,208},{224,240}..., dimensions={0}, use_global_device_ids=true | all-gather | bytes 49152 | tf_op jit(solution)/shard_map/all_gather | solution.py:288
  91.1 20.4 %all_to_all.10 = f32[16,16,128]{2,1,0:T(8,128)S(1)} all-to-all(f32[16,16,128]{2,1,0:T(8,128)S(1)} %broadcast_in_dim.10), channel_id=1, replica_groups={{0,32,64,96,128,160,192,224,256,288,320,352,384,416,448,480},{16,48,80,..., dimensions={0} | all-to-all | bytes 262144 | tf_op jit(solution)/shard_map/all_to_all | solution.py:293
  111.5 4.9 %all_gather.11.gram_ref = f32[32,128]{1,0:T(8,128)} all-gather(f32[16,128]{1,0:T(8,128)S(1)} %reduce_sum.29), channel_id=1, replica_groups={{0,16},{32,48},{64,80},{96,112},{128,144},{160,176},{192,208},{224,240}..., dimensions={0}, use_global_device_ids=true | all-gather | bytes 24576 | tf_op jit(solution)/shard_map/all_gather | solution.py:294
  116.4 8.6 %shard_map.62 = (f32[64,4096]{1,0:T(8,128)}, f32[64,64]{1,0:T(8,128)}) custom-call(f32[32,128]{1,0:T(8,128)} %all_gather.11.gram_ref, f32[64,4096]{1,0:T(8,128)} %get-tuple-element.9.image_ref), custom_call_target="tpu_custom_call" | custom-call | tf_op jit(solution)/shard_map/pallas_call | solution.py:324
  (5 shorter events, 0.1 us)
Async XLA Ops:
  5.4 17.2 %collective-permute-start = (bf16[64,1024]{1,0:T(8,128)(2,1)}, bf16[64,1024]{1,0:T(8,128)(2,1)S(1)}, u32[]{:S(2)}, u32[]{:S(2)}) collective-permute-start(bf16[64,1024]{1,0:T(8,128)(2,1)} %get-tuple-element.6), channel_id=1, source_target_pairs={{0,1},{1,2},{2,3},{3,4},{4,5},{5,6},{6,7},{7,8},{8,9},{9,10},{10,1... | collective-permute-start | bytes 393224 | tf_op jit(solution)/shard_map/ppermute | solution.py:24
  9.3 13.3 %collective-permute-start.1 = (bf16[64,1024]{1,0:T(8,128)(2,1)}, bf16[64,1024]{1,0:T(8,128)(2,1)S(1)}, u32[]{:S(2)}, u32[]{:S(2)}) collective-permute-start(bf16[64,1024]{1,0:T(8,128)(2,1)} %get-tuple-element.7), channel_id=1, source_target_pairs={{0,511},{1,0},{2,1},{3,2},{4,3},{5,4},{6,5},{7,6},{8,7},{9,8},{10,... | collective-permute-start | bytes 393224 | tf_op jit(solution)/shard_map/ppermute | solution.py:24
  22.6 0.6 copy-start
  22.6 0.7 copy-start.1
  68.5 11.8 %all-to-all-start = ((f32[16,32,128]{2,1,0:T(8,128)}), f32[16,32,128]{2,1,0:T(8,128)S(1)}, u32[]{:S(2)}, u32[]{:S(2)}) async-start(f32[16,32,128]{2,1,0:T(8,128)} %get-tuple-element.8), calls=%async_computation | async-start | bytes 524288 | tf_op jit(solution)/shard_map/all_to_all | solution.py:287

commit v3 on v2

--- a/solution.py
+++ b/solution.py
@@ -11,10 +11,10 @@
 HIGHEST = lax.Precision.HIGHEST
 BLOCK = 512
 CHUNK = 256
-FIELDS = 4
+FIELDS = 8
 PICK = 512
 SPAN = 4096
-AHEAD = 2
+GROUP = 8
 VMEM_LIMIT = 60 << 20
 
 
@@ -68,13 +68,23 @@
     )(halo_rows, vectors)
 
 
-def spread_pins(stride, pins, place_tile, value_tile):
+def ranks(pins):
+    rows = [jnp.zeros_like(pins[:1])]
+    for slot in range(1, pins.shape[0]):
+        same = (pins[:slot] == pins[slot : slot + 1]).astype(jnp.int32)
+        rows.append(jnp.sum(same, axis=0, keepdims=True))
+    return jnp.concatenate(rows, axis=0)
+
+
+def spread_pins(stride, turn, pins, place_tile, value_tile):
     slots, block = pins.shape
     field = jnp.zeros(pins.shape, jnp.int32)
     for index in range(1, FIELDS):
         field = field + (pins >= index * stride).astype(jnp.int32)
-    place = pins - field * stride
-    value = jnp.where(field == 0, 1, jnp.where(field == 1, 16, jnp.where(field == 2, 256, 4096)))
+    rank = ranks(pins)
+    mine = (rank >= 3 * turn) & (rank < 3 * turn + 3)
+    place = jnp.where(mine, pins - field * stride, -1)
+    value = lax.shift_left(jnp.ones_like(field), 2 * field)
     for slot in range(slots):
         place_tile[slot] = jnp.broadcast_to(place[slot : slot + 1, :], (16, block)).astype(jnp.int16)
         value_tile[slot] = jnp.broadcast_to(value[slot : slot + 1, :], (16, block)).astype(jnp.int16)
@@ -94,22 +104,26 @@
     return jnp.concatenate(rows, axis=0)
 
 
+def unpack(words, field):
+    return (lax.shift_right_logical(words, jnp.int16(2 * field)) & jnp.int16(3)).astype(jnp.bfloat16)
+
+
 def words_kernel(pins_ref, words_ref, place_tile, value_tile):
     stride = words_ref.shape[0]
-    spread_pins(stride, pins_ref[...], place_tile, value_tile)
+    extent = stride // 2
+    spread_pins(stride, 0, pins_ref[...], place_tile, value_tile)
 
     def step(chunk, carry):
-        words_ref[pl.ds(pl.multiple_of(chunk * 512, 512), 512), :] = build_words(
-            chunk, 512, place_tile, value_tile
+        words_ref[pl.ds(pl.multiple_of(chunk * extent, extent), extent), :] = build_words(
+            chunk, extent, place_tile, value_tile
         )
         return carry
 
-    lax.fori_loop(0, stride // 512, step, 0)
+    lax.fori_loop(0, stride // extent, step, 0)
 
 
 def count_words(pins, total):
-    slots = pins.shape[0]
-    nets = 2 * BLOCK * AHEAD
+    slots, nets = pins.shape
     stride = total // FIELDS
     return pl.pallas_call(
         words_kernel,
@@ -151,12 +165,12 @@
         parts = jnp.where(row == 0, first, jnp.where(row == 1, second, jnp.where(row == 2, third, 0.0)))
         target[width:, :] = parts.astype(jnp.bfloat16)
 
-    def step(half, unpack, spread, owned, ahead, chunk):
-        base = pl.multiple_of(chunk * CHUNK, CHUNK)
+    def step(half, gather, spread, owned, chunk):
+        base = chunk * CHUNK
         added = []
         if spread is not None:
             for field in range(owned):
-                place = pl.multiple_of(field * stride + base, CHUNK)
+                place = field * stride + base
                 added.append(
                     lax.dot_general(
                         scaled[spread][...],
@@ -165,16 +179,12 @@
                         preferred_element_type=jnp.float32,
                     )
                 )
-        if unpack:
-            if ahead:
-                words = words_ref[pl.ds(base, CHUNK), half * BLOCK : (half + 1) * BLOCK]
-            else:
-                words = build_words(chunk, CHUNK, place_tile, value_tile)
+        if gather:
+            words = words_ref[pl.ds(base, CHUNK), half * BLOCK : (half + 1) * BLOCK]
             fresh = jnp.zeros(sums.shape, jnp.float32)
             for field in range(FIELDS):
-                place = pl.multiple_of(field * stride + base, CHUNK)
-                tile = lax.shift_right_logical(words, jnp.int16(4 * field)) & jnp.int16(15)
-                tile = tile.astype(jnp.bfloat16)
+                place = field * stride + base
+                tile = unpack(words, field)
                 if field < owned:
                     incs[half][pl.ds(place, CHUNK), :] = tile
                 fresh = fresh + jnp.dot(
@@ -182,28 +192,52 @@
                 )
             sums[...] += fresh
         for field, term in enumerate(added):
+            place = field * stride + base
+            contrib[:, pl.ds(place, CHUNK)] += term
+
+    def repeats(half, owned, chunk):
+        base = pl.multiple_of(chunk * CHUNK, CHUNK)
+        words = build_words(chunk, CHUNK, place_tile, value_tile)
+        for field in range(FIELDS):
             place = pl.multiple_of(field * stride + base, CHUNK)
-            contrib[:, pl.ds(place, CHUNK)] += term
-
-    def sweep(half, unpack, spread, ahead):
-        if unpack and not ahead:
-            spread_pins(stride, pins_ref[:, half * BLOCK : (half + 1) * BLOCK], place_tile, value_tile)
-        if unpack:
-            sums[...] = jnp.zeros_like(sums)
-        many = -(-cells // stride)
-        edge = (cells - (many - 1) * stride) // CHUNK
-
+            tile = unpack(words, field)
+            if field < owned:
+                incs[half][pl.ds(place, CHUNK), :] += tile
+            sums[...] += jnp.dot(extended[:, pl.ds(place, CHUNK)], tile, preferred_element_type=jnp.float32)
+
+    many = -(-cells // stride)
+    edge = (cells - (many - 1) * stride) // CHUNK
+
+    def over_chunks(work):
         def low(chunk, carry):
-            step(half, unpack, spread, many, ahead, chunk)
+            work(many, chunk)
             return carry
 
         def high(chunk, carry):
-            step(half, unpack, spread, many - 1, ahead, chunk)
+            work(many - 1, chunk)
             return carry
 
         lax.fori_loop(0, edge, low, 0)
         lax.fori_loop(edge, stride // CHUNK, high, 0)
-        if unpack:
+
+    def sweep(half, gather, spread):
+        if gather:
+            sums[...] = jnp.zeros_like(sums)
+        for chunk in range(stride // CHUNK):
+            step(half, gather, spread, many if chunk < edge else many - 1, chunk)
+        if gather:
+            pins = pins_ref[:, half * BLOCK : (half + 1) * BLOCK]
+            most = jnp.max(jnp.where(pins >= 0, ranks(pins), 0))
+
+            @pl.when(most >= 3)
+            def _():
+                def again(later, carry):
+                    spread_pins(stride, later, pins, place_tile, value_tile)
+                    over_chunks(functools.partial(repeats, half))
+                    return carry
+
+                lax.fori_loop(1, 3, again, 0)
+
             finish(half)
 
     @pl.when(turn == 0)
@@ -212,27 +246,17 @@
         extended[:, cells : cells + bound] = prev_ref[...]
         extended[:, cells + bound :] = next_ref[...]
         contrib[...] = jnp.zeros_like(contrib)
-        sweep(0, True, None, AHEAD > 0)
-
-    @pl.when((turn > 0) & (turn < AHEAD))
+        sweep(0, True, None)
+
+    @pl.when(turn > 0)
     def _():
-        sweep(0, True, 1, True)
-
-    @pl.when((turn > 0) & (turn >= AHEAD))
-    def _():
-        sweep(0, True, 1, False)
-
-    @pl.when(turn < AHEAD)
-    def _():
-        sweep(1, True, 0, True)
-
-    @pl.when(turn >= AHEAD)
-    def _():
-        sweep(1, True, 0, False)
+        sweep(0, True, 1)
+
+    sweep(1, True, 0)
 
     @pl.when(turn == pl.num_programs(0) - 1)
     def _():
-        sweep(1, False, 1, True)
+        sweep(1, False, 1)
         degree = (
             contrib[width : width + 1, :] + contrib[width + 1 : width + 2, :] + contrib[width + 2 : width + 3, :]
         )
@@ -260,7 +284,7 @@
             jax.ShapeDtypeStruct((copies, width // 2, 2 * width), jnp.float32),
         ),
         in_specs=[
-            pl.BlockSpec((stride, 2 * BLOCK), lambda step: (0, jnp.minimum(step, AHEAD - 1))),
+            pl.BlockSpec((stride, 2 * BLOCK), lambda step: (0, step)),
             pl.BlockSpec((slots, 2 * BLOCK), lambda step: (0, step)),
         ]
         + [whole] * 4,
@@ -302,14 +326,25 @@
     unit = (columns == rows + width).astype(jnp.float32)
     work = jnp.concatenate([gram, jnp.zeros((width, width), jnp.float32)], axis=1) + unit
     pivots = []
-    for index in range(width):
+    for index in range(0, width, GROUP):
         base = index // 8 * 8
         part = work[base:]
-        row = work[index : index + 1]
-        pivot = work[index : index + 1, index : index + 1]
-        pivots.append(pivot)
-        column = jnp.where(rows[base:] > index, part[:, index : index + 1], 0.0)
-        part = part - column * (row * (1.0 / pivot))
+        below = rows[base:]
+        first = index - base
+        spread = [jnp.broadcast_to(part[:, index + item : index + item + 1], part.shape) for item in range(GROUP)]
+        lines = [part[first + item : first + item + 1] for item in range(GROUP)]
+        for item in range(GROUP):
+            here = first + item
+            pivot = spread[item][here : here + 1]
+            pivots.append(pivot)
+            inverse = 1.0 / pivot
+            column = jnp.where(below > index + item, spread[item], 0.0)
+            line = lines[item] * inverse
+            for other in range(item + 1, GROUP):
+                ratio = spread[other][here : here + 1] * inverse
+                spread[other] = spread[other] - column * ratio
+                lines[other] = lines[other] - column[first + other : first + other + 1] * line
+            part = part - column * line
         work = jnp.concatenate([work[:base], part], axis=0) if base else part
     work = work / jnp.sqrt(jnp.concatenate(pivots, axis=0))
     upper = columns[:, :width] >= rows[:, :width]

time: 126 us -> 115 us (0.913)
  Pallas kernels: 65.7 us -> 55 us
    pallas_call x1, Pallas kernels: 45.3 us -> 35.7 us  [image_and_gram(): pl.pallas_call(image_kernel, grid=(nets // (2 * BLOCK),), out_shape=(jax....]
    pallas_call x1, Pallas kernels: 8.63 us -> 4.74 us  [factor_and_embed(): pl.pallas_call(functools.partial(factor_kernel, scale), out_shape=(jax.Sh...]
    pallas_call x1, Pallas kernels: 7.08 us -> 9.85 us  [count_words(): pl.pallas_call(words_kernel, grid=(nets // BLOCK,), out_shape=jax.ShapeDt...]
  transfers between devices with their start and end apart: 3 -> 3, of which waited for: 1 -> 1; matrix products, arithmetic and copies ran while one was open for 0% -> 0% of each run, Pallas kernels for 6% -> 9%
where the time goes in v3:
time: 115 us; the launch traced here: 114 us
  Pallas kernels  55 us (48%)
  blocking collectives  36.7 us (32%)
  starting transfers between devices  13.7 us (12%)
  waiting for transfers between devices  7.5 us (7%)
    pallas_call x1, Pallas kernels, image_and_gram(): pl.pallas_call(image_kernel, grid=(nets // (2 * BLOCK),), out_shape=(jax....  35.7 us
    all_to_all x1, blocking collectives, summed_gram(): lax.all_to_all(share, 'wide', 0, 0, axis_index_groups=columns)  20.4 us
    all_gather x1, blocking collectives, summed_gram(): lax.all_gather(plane, 'wide', axis_index_groups=pairs)  11.4 us
    ppermute x2, starting transfers between devices, shifted(): return lax.ppermute(value, BOTH, pairs)  10.1 us
    pallas_call x1, Pallas kernels, count_words(): pl.pallas_call(words_kernel, grid=(nets // BLOCK,), out_shape=jax.ShapeDt...  9.85 us
    all_to_all x1, waiting for transfers between devices, summed_gram(): plane = jnp.sum(lax.all_to_all(copies, 'narrow', 0, 0), axis=0)  7.49 us
    all_gather x1, blocking collectives, summed_gram(): return lax.all_gather(share, 'wide', axis_index_groups=pairs, tiled=True)  4.86 us
    pallas_call x1, Pallas kernels, factor_and_embed(): pl.pallas_call(functools.partial(factor_kernel, scale), out_shape=(jax.Sh...  4.74 us
  transfers between devices with their start and end apart: 3, of which 1 were waited for; matrix products, arithmetic and copies ran while one was open for 0% of the time, Pallas kernels for 9%

profile of v3, /device:TPU:1, one launch (start us, length us, event | category | flops | bytes accessed | tf_op | source)
XLA Modules:
  0.0 114.3 jit_solution(2722156035475630497)
XLA Ops:
  0.6 4.7 %shard_map.60 = (bf16[64,1024]{1,0:T(8,128)(2,1)}, bf16[64,1024]{1,0:T(8,128)(2,1)}) custom-call(s32[2,1024]{1,0:T(2,128)} %rows_ref.1, bf16[64,4096]{1,0:T(8,128)(2,1)} %vectors_ref.3), custom_call_target="tpu_custom_call" | custom-call | flops 1073741824 | bytes 524288 | tf_op jit(solution)/shard_map/pallas_call | solution.py:59
  5.4 3.9 %collective-permute-start = (bf16[64,1024]{1,0:T(8,128)(2,1)}, bf16[64,1024]{1,0:T(8,128)(2,1)S(1)}, u32[]{:S(2)}, u32[]{:S(2)}) collective-permute-start(bf16[64,1024]{1,0:T(8,128)(2,1)} %get-tuple-element.6), channel_id=1, source_target_pairs={{0,1},{1,2},{2,3},{3,4},{4,5},{5,6},{6,7},{7,8},{8,9},{9,10},{10,1... | collective-permute-start | bytes 393224 | tf_op jit(solution)/shard_map/ppermute | solution.py:24
  9.3 6.2 %collective-permute-start.1 = (bf16[64,1024]{1,0:T(8,128)(2,1)}, bf16[64,1024]{1,0:T(8,128)(2,1)S(1)}, u32[]{:S(2)}, u32[]{:S(2)}) collective-permute-start(bf16[64,1024]{1,0:T(8,128)(2,1)} %get-tuple-element.7), channel_id=1, source_target_pairs={{0,511},{1,0},{2,1},{3,2},{4,3},{5,4},{6,5},{7,6},{8,7},{9,8},{10,... | collective-permute-start | bytes 393224 | tf_op jit(solution)/shard_map/ppermute | solution.py:24
  15.5 9.8 %shard_map.59.words_ref = s16[768,5120]{1,0:T(8,128)(2,1)} custom-call(s32[8,5120]{1,0:T(8,128)} %pins_ref.3), custom_call_target="tpu_custom_call" | custom-call | flops 94371840 | bytes 7864320 | tf_op jit(solution)/shard_map/pallas_call | solution.py:128
  25.4 0.0 collective-permute-done.prev_ref
  25.4 0.0 copy-start
  25.4 0.0 collective-permute-done.1.next_ref
  25.4 0.0 copy-start.1
  25.4 0.6 copy-done
  26.0 0.1 copy-done.1
  26.1 35.7 %shard_map.61 = (f32[64,4096]{1,0:T(8,128)}, f32[16,32,128]{2,1,0:T(8,128)}) custom-call(s16[768,5120]{1,0:T(8,128)(2,1)} %shard_map.59.words_ref, s32[8,5120]{1,0:T(8,128)} %pins_ref.3, bf16[64,4096]{1,0:T(8,128)(2,1)} %vectors_ref.3, bf16[64,1024]{1,0:T(8,128)(2,1)} %copy-done, bf16[64,1024]{1,0:T(8,128)(2,1)} %copy-done.1, f32[1,4096]{1,0:T(1,128)} %bitcast.3), custom_call_target="tpu_custom_call" | custom-call | tf_op jit(solution)/shard_map/pallas_call | solution.py:279
  61.8 3.5 %all-to-all-start = ((f32[16,32,128]{2,1,0:T(8,128)}), f32[16,32,128]{2,1,0:T(8,128)S(1)}, u32[]{:S(2)}, u32[]{:S(2)}) async-start(f32[16,32,128]{2,1,0:T(8,128)} %get-tuple-element.8), calls=%async_computation | async-start | bytes 524288 | tf_op jit(solution)/shard_map/all_to_all | solution.py:311
  65.3 7.5 %all-to-all-done = f32[16,32,128]{2,1,0:T(8,128)S(1)} async-done(((f32[16,32,128]{2,1,0:T(8,128)}), f32[16,32,128]{2,1,0:T(8,128)S(1)}, u32[]{:S(2)}, u32[]{:S(2)}) %all-to-all-start) | async-done | bytes 262176 | tf_op jit(solution)/shard_map/all_to_all | solution.py:311
  72.8 11.4 %all-gather = f32[64,128]{1,0:T(8,128)S(1)} all-gather(f32[32,128]{1,0:T(8,128)S(1)} %reduce_sum.27), channel_id=2, replica_groups={{0,16},{32,48},{64,80},{96,112},{128,144},{160,176},{192,208},{224,240}..., dimensions={0}, use_global_device_ids=true | all-gather | bytes 49152 | tf_op jit(solution)/shard_map/all_gather | solution.py:312
  84.3 20.4 %all_to_all.10 = f32[16,16,128]{2,1,0:T(8,128)S(1)} all-to-all(f32[16,16,128]{2,1,0:T(8,128)S(1)} %broadcast_in_dim.10), channel_id=1, replica_groups={{0,32,64,96,128,160,192,224,256,288,320,352,384,416,448,480},{16,48,80,..., dimensions={0} | all-to-all | bytes 262144 | tf_op jit(solution)/shard_map/all_to_all | solution.py:317
  104.7 4.9 %all_gather.11.gram_ref = f32[32,128]{1,0:T(8,128)} all-gather(f32[16,128]{1,0:T(8,128)S(1)} %reduce_sum.29), channel_id=1, replica_groups={{0,16},{32,48},{64,80},{96,112},{128,144},{160,176},{192,208},{224,240}..., dimensions={0}, use_global_device_ids=true | all-gather | bytes 24576 | tf_op jit(solution)/shard_map/all_gather | solution.py:318
  109.6 4.7 %shard_map.62 = (f32[64,4096]{1,0:T(8,128)}, f32[64,64]{1,0:T(8,128)}) custom-call(f32[32,128]{1,0:T(8,128)} %all_gather.11.gram_ref, f32[64,4096]{1,0:T(8,128)} %get-tuple-element.9.image_ref), custom_call_target="tpu_custom_call" | custom-call | tf_op jit(solution)/shard_map/pallas_call | solution.py:359
  (5 shorter events, 0.1 us)
Async XLA Ops:
  5.4 20.0 %collective-permute-start = (bf16[64,1024]{1,0:T(8,128)(2,1)}, bf16[64,1024]{1,0:T(8,128)(2,1)S(1)}, u32[]{:S(2)}, u32[]{:S(2)}) collective-permute-start(bf16[64,1024]{1,0:T(8,128)(2,1)} %get-tuple-element.6), channel_id=1, source_target_pairs={{0,1},{1,2},{2,3},{3,4},{4,5},{5,6},{6,7},{7,8},{8,9},{9,10},{10,1... | collective-permute-start | bytes 393224 | tf_op jit(solution)/shard_map/ppermute | solution.py:24
  9.3 16.1 %collective-permute-start.1 = (bf16[64,1024]{1,0:T(8,128)(2,1)}, bf16[64,1024]{1,0:T(8,128)(2,1)S(1)}, u32[]{:S(2)}, u32[]{:S(2)}) collective-permute-start(bf16[64,1024]{1,0:T(8,128)(2,1)} %get-tuple-element.7), channel_id=1, source_target_pairs={{0,511},{1,0},{2,1},{3,2},{4,3},{5,4},{6,5},{7,6},{8,7},{9,8},{10,... | collective-permute-start | bytes 393224 | tf_op jit(solution)/shard_map/ppermute | solution.py:24
  25.4 0.7 copy-start
  25.4 0.7 copy-start.1
  61.8 11.0 %all-to-all-start = ((f32[16,32,128]{2,1,0:T(8,128)}), f32[16,32,128]{2,1,0:T(8,128)S(1)}, u32[]{:S(2)}, u32[]{:S(2)}) async-start(f32[16,32,128]{2,1,0:T(8,128)} %get-tuple-element.8), calls=%async_computation | async-start | bytes 524288 | tf_op jit(solution)/shard_map/all_to_all | solution.py:311

commit v4 on v3

--- a/solution.py
+++ b/solution.py
@@ -167,33 +167,27 @@
 
     def step(half, gather, spread, owned, chunk):
         base = chunk * CHUNK
-        added = []
-        if spread is not None:
-            for field in range(owned):
-                place = field * stride + base
-                added.append(
-                    lax.dot_general(
-                        scaled[spread][...],
-                        incs[spread][pl.ds(place, CHUNK), :],
-                        (((1,), (1,)), ((), ())),
-                        preferred_element_type=jnp.float32,
-                    )
-                )
         if gather:
             words = words_ref[pl.ds(base, CHUNK), half * BLOCK : (half + 1) * BLOCK]
             fresh = jnp.zeros(sums.shape, jnp.float32)
-            for field in range(FIELDS):
-                place = field * stride + base
+        for field in range(FIELDS):
+            place = field * stride + base
+            if spread is not None and field < owned:
+                contrib[:, pl.ds(place, CHUNK)] += lax.dot_general(
+                    scaled[spread][...],
+                    incs[spread][pl.ds(place, CHUNK), :],
+                    (((1,), (1,)), ((), ())),
+                    preferred_element_type=jnp.float32,
+                )
+            if gather:
                 tile = unpack(words, field)
                 if field < owned:
                     incs[half][pl.ds(place, CHUNK), :] = tile
                 fresh = fresh + jnp.dot(
                     extended[:, pl.ds(place, CHUNK)], tile, preferred_element_type=jnp.float32
                 )
+        if gather:
             sums[...] += fresh
-        for field, term in enumerate(added):
-            place = field * stride + base
-            contrib[:, pl.ds(place, CHUNK)] += term
 
     def repeats(half, owned, chunk):
         base = pl.multiple_of(chunk * CHUNK, CHUNK)

time: 115 us -> 110 us (0.957)
  Pallas kernels: 55 us -> 50.5 us
    pallas_call x1, Pallas kernels: 35.7 us -> 31.2 us  [image_and_gram(): pl.pallas_call(image_kernel, grid=(nets // (2 * BLOCK),), out_shape=(jax....]
where the time goes in v4:
time: 110 us
  Pallas kernels  50.5 us (46%)
  blocking collectives  36.7 us (33%)
  starting transfers between devices  13.7 us (12%)
  waiting for transfers between devices  7.5 us (7%)
    pallas_call x1, Pallas kernels, image_and_gram(): pl.pallas_call(image_kernel, grid=(nets // (2 * BLOCK),), out_shape=(jax....  31.2 us
    all_to_all x1, blocking collectives, summed_gram(): lax.all_to_all(share, 'wide', 0, 0, axis_index_groups=columns)  20.4 us
    all_gather x1, blocking collectives, summed_gram(): lax.all_gather(plane, 'wide', axis_index_groups=pairs)  11.4 us
    ppermute x2, starting transfers between devices, shifted(): return lax.ppermute(value, BOTH, pairs)  10.1 us
    pallas_call x1, Pallas kernels, count_words(): pl.pallas_call(words_kernel, grid=(nets // BLOCK,), out_shape=jax.ShapeDt...  9.85 us
    all_to_all x1, waiting for transfers between devices, summed_gram(): plane = jnp.sum(lax.all_to_all(copies, 'narrow', 0, 0), axis=0)  7.49 us
    all_gather x1, blocking collectives, summed_gram(): return lax.all_gather(share, 'wide', axis_index_groups=pairs, tiled=True)  4.86 us
    pallas_call x1, Pallas kernels, factor_and_embed(): pl.pallas_call(functools.partial(factor_kernel, scale), out_shape=(jax.Sh...  4.75 us
  transfers between devices with their start and end apart: 3, of which 1 were waited for; matrix products, arithmetic and copies ran while one was open for 0% of the time, Pallas kernels for 9%

profile of v4, /device:TPU:1, one launch (start us, length us, event | category | flops | bytes accessed | tf_op | source)
XLA Modules:
  0.0 109.9 jit_solution(683381403721208858)
XLA Ops:
  0.6 4.7 %shard_map.60 = (bf16[64,1024]{1,0:T(8,128)(2,1)}, bf16[64,1024]{1,0:T(8,128)(2,1)}) custom-call(s32[2,1024]{1,0:T(2,128)} %rows_ref.1, bf16[64,4096]{1,0:T(8,128)(2,1)} %vectors_ref.3), custom_call_target="tpu_custom_call" | custom-call | flops 1073741824 | bytes 524288 | tf_op jit(solution)/shard_map/pallas_call | solution.py:59
  5.4 3.9 %collective-permute-start = (bf16[64,1024]{1,0:T(8,128)(2,1)}, bf16[64,1024]{1,0:T(8,128)(2,1)S(1)}, u32[]{:S(2)}, u32[]{:S(2)}) collective-permute-start(bf16[64,1024]{1,0:T(8,128)(2,1)} %get-tuple-element.6), channel_id=1, source_target_pairs={{0,1},{1,2},{2,3},{3,4},{4,5},{5,6},{6,7},{7,8},{8,9},{9,10},{10,1... | collective-permute-start | bytes 393224 | tf_op jit(solution)/shard_map/ppermute | solution.py:24
  9.3 6.2 %collective-permute-start.1 = (bf16[64,1024]{1,0:T(8,128)(2,1)}, bf16[64,1024]{1,0:T(8,128)(2,1)S(1)}, u32[]{:S(2)}, u32[]{:S(2)}) collective-permute-start(bf16[64,1024]{1,0:T(8,128)(2,1)} %get-tuple-element.7), channel_id=1, source_target_pairs={{0,511},{1,0},{2,1},{3,2},{4,3},{5,4},{6,5},{7,6},{8,7},{9,8},{10,... | collective-permute-start | bytes 393224 | tf_op jit(solution)/shard_map/ppermute | solution.py:24
  15.5 9.8 %shard_map.59.words_ref = s16[768,5120]{1,0:T(8,128)(2,1)} custom-call(s32[8,5120]{1,0:T(8,128)} %pins_ref.3), custom_call_target="tpu_custom_call" | custom-call | flops 94371840 | bytes 7864320 | tf_op jit(solution)/shard_map/pallas_call | solution.py:128
  25.4 0.0 collective-permute-done.prev_ref
  25.4 0.0 copy-start
  25.4 0.0 collective-permute-done.1.next_ref
  25.4 0.0 copy-start.1
  25.4 0.6 copy-done
  26.0 0.1 copy-done.1
  26.1 31.2 %shard_map.61 = (f32[64,4096]{1,0:T(8,128)}, f32[16,32,128]{2,1,0:T(8,128)}) custom-call(s16[768,5120]{1,0:T(8,128)(2,1)} %shard_map.59.words_ref, s32[8,5120]{1,0:T(8,128)} %pins_ref.3, bf16[64,4096]{1,0:T(8,128)(2,1)} %vectors_ref.3, bf16[64,1024]{1,0:T(8,128)(2,1)} %copy-done, bf16[64,1024]{1,0:T(8,128)(2,1)} %copy-done.1, f32[1,4096]{1,0:T(1,128)} %bitcast.3), custom_call_target="tpu_custom_call" | custom-call | tf_op jit(solution)/shard_map/pallas_call | solution.py:273
  57.3 3.5 %all-to-all-start = ((f32[16,32,128]{2,1,0:T(8,128)}), f32[16,32,128]{2,1,0:T(8,128)S(1)}, u32[]{:S(2)}, u32[]{:S(2)}) async-start(f32[16,32,128]{2,1,0:T(8,128)} %get-tuple-element.8), calls=%async_computation | async-start | bytes 524288 | tf_op jit(solution)/shard_map/all_to_all | solution.py:305
  60.8 7.5 %all-to-all-done = f32[16,32,128]{2,1,0:T(8,128)S(1)} async-done(((f32[16,32,128]{2,1,0:T(8,128)}), f32[16,32,128]{2,1,0:T(8,128)S(1)}, u32[]{:S(2)}, u32[]{:S(2)}) %all-to-all-start) | async-done | bytes 262176 | tf_op jit(solution)/shard_map/all_to_all | solution.py:305
  68.4 11.4 %all-gather = f32[64,128]{1,0:T(8,128)S(1)} all-gather(f32[32,128]{1,0:T(8,128)S(1)} %reduce_sum.27), channel_id=2, replica_groups={{0,16},{32,48},{64,80},{96,112},{128,144},{160,176},{192,208},{224,240}..., dimensions={0}, use_global_device_ids=true | all-gather | bytes 49152 | tf_op jit(solution)/shard_map/all_gather | solution.py:306
  79.8 20.4 %all_to_all.10 = f32[16,16,128]{2,1,0:T(8,128)S(1)} all-to-all(f32[16,16,128]{2,1,0:T(8,128)S(1)} %broadcast_in_dim.10), channel_id=1, replica_groups={{0,32,64,96,128,160,192,224,256,288,320,352,384,416,448,480},{16,48,80,..., dimensions={0} | all-to-all | bytes 262144 | tf_op jit(solution)/shard_map/all_to_all | solution.py:311
  100.3 4.9 %all_gather.11.gram_ref = f32[32,128]{1,0:T(8,128)} all-gather(f32[16,128]{1,0:T(8,128)S(1)} %reduce_sum.29), channel_id=1, replica_groups={{0,16},{32,48},{64,80},{96,112},{128,144},{160,176},{192,208},{224,240}..., dimensions={0}, use_global_device_ids=true | all-gather | bytes 24576 | tf_op jit(solution)/shard_map/all_gather | solution.py:312
  105.1 4.7 %shard_map.62 = (f32[64,4096]{1,0:T(8,128)}, f32[64,64]{1,0:T(8,128)}) custom-call(f32[32,128]{1,0:T(8,128)} %all_gather.11.gram_ref, f32[64,4096]{1,0:T(8,128)} %get-tuple-element.9.image_ref), custom_call_target="tpu_custom_call" | custom-call | tf_op jit(solution)/shard_map/pallas_call | solution.py:353
  (5 shorter events, 0.1 us)
Async XLA Ops:
  5.4 20.0 %collective-permute-start = (bf16[64,1024]{1,0:T(8,128)(2,1)}, bf16[64,1024]{1,0:T(8,128)(2,1)S(1)}, u32[]{:S(2)}, u32[]{:S(2)}) collective-permute-start(bf16[64,1024]{1,0:T(8,128)(2,1)} %get-tuple-element.6), channel_id=1, source_target_pairs={{0,1},{1,2},{2,3},{3,4},{4,5},{5,6},{6,7},{7,8},{8,9},{9,10},{10,1... | collective-permute-start | bytes 393224 | tf_op jit(solution)/shard_map/ppermute | solution.py:24
  9.3 16.1 %collective-permute-start.1 = (bf16[64,1024]{1,0:T(8,128)(2,1)}, bf16[64,1024]{1,0:T(8,128)(2,1)S(1)}, u32[]{:S(2)}, u32[]{:S(2)}) collective-permute-start(bf16[64,1024]{1,0:T(8,128)(2,1)} %get-tuple-element.7), channel_id=1, source_target_pairs={{0,511},{1,0},{2,1},{3,2},{4,3},{5,4},{6,5},{7,6},{8,7},{9,8},{10,... | collective-permute-start | bytes 393224 | tf_op jit(solution)/shard_map/ppermute | solution.py:24
  25.4 0.7 copy-start
  25.4 0.7 copy-start.1
  57.3 11.0 %all-to-all-start = ((f32[16,32,128]{2,1,0:T(8,128)}), f32[16,32,128]{2,1,0:T(8,128)S(1)}, u32[]{:S(2)}, u32[]{:S(2)}) async-start(f32[16,32,128]{2,1,0:T(8,128)} %get-tuple-element.8), calls=%async_computation | async-start | bytes 524288 | tf_op jit(solution)/shard_map/all_to_all | solution.py:305

commit v5 on v4

--- a/solution.py
+++ b/solution.py
@@ -15,6 +15,7 @@
 PICK = 512
 SPAN = 4096
 GROUP = 8
+WIDE = 1024
 VMEM_LIMIT = 60 << 20
 
 
@@ -127,11 +128,11 @@
     stride = total // FIELDS
     return pl.pallas_call(
         words_kernel,
-        grid=(nets // BLOCK,),
+        grid=(nets // WIDE,),
         out_shape=jax.ShapeDtypeStruct((stride, nets), jnp.int16),
-        in_specs=[pl.BlockSpec((slots, BLOCK), lambda step: (0, step))],
-        out_specs=pl.BlockSpec((stride, BLOCK), lambda step: (0, step)),
-        scratch_shapes=[pltpu.VMEM((slots, 16, BLOCK), jnp.int16)] * 2,
+        in_specs=[pl.BlockSpec((slots, WIDE), lambda step: (0, step))],
+        out_specs=pl.BlockSpec((stride, WIDE), lambda step: (0, step)),
+        scratch_shapes=[pltpu.VMEM((slots, 16, WIDE), jnp.int16)] * 2,
         cost_estimate=pl.CostEstimate(
             flops=24 * stride * nets, bytes_accessed=2 * stride * nets, transcendentals=0
         ),
@@ -169,7 +170,6 @@
         base = chunk * CHUNK
         if gather:
             words = words_ref[pl.ds(base, CHUNK), half * BLOCK : (half + 1) * BLOCK]
-            fresh = jnp.zeros(sums.shape, jnp.float32)
         for field in range(FIELDS):
             place = field * stride + base
             if spread is not None and field < owned:
@@ -183,11 +183,7 @@
                 tile = unpack(words, field)
                 if field < owned:
                     incs[half][pl.ds(place, CHUNK), :] = tile
-                fresh = fresh + jnp.dot(
-                    extended[:, pl.ds(place, CHUNK)], tile, preferred_element_type=jnp.float32
-                )
-        if gather:
-            sums[...] += fresh
+                sums[...] += jnp.dot(extended[:, pl.ds(place, CHUNK)], tile, preferred_element_type=jnp.float32)
 
     def repeats(half, owned, chunk):
         base = pl.multiple_of(chunk * CHUNK, CHUNK)

time: 110 us -> 108 us (0.982)
  Pallas kernels: 50.5 us -> 48 us
    pallas_call x1, Pallas kernels: 31.2 us -> 29.7 us  [image_and_gram(): pl.pallas_call(image_kernel, grid=(nets // (2 * BLOCK),), out_shape=(jax....]
  transfers between devices with their start and end apart: 3 -> 3, of which waited for: 1 -> 1; matrix products, arithmetic and copies ran while one was open for 0% -> 0% of each run, Pallas kernels for 9% -> 8%
where the time goes in v5:
time: 108 us; the launch traced here: 107 us
  Pallas kernels  48 us (44%)
  blocking collectives  36.7 us (34%)
  starting transfers between devices  13.7 us (13%)
  waiting for transfers between devices  7.5 us (7%)
    pallas_call x1, Pallas kernels, image_and_gram(): pl.pallas_call(image_kernel, grid=(nets // (2 * BLOCK),), out_shape=(jax....  29.7 us
    all_to_all x1, blocking collectives, summed_gram(): lax.all_to_all(share, 'wide', 0, 0, axis_index_groups=columns)  20.4 us
    all_gather x1, blocking collectives, summed_gram(): lax.all_gather(plane, 'wide', axis_index_groups=pairs)  11.4 us
    ppermute x2, starting transfers between devices, shifted(): return lax.ppermute(value, BOTH, pairs)  10.1 us
    pallas_call x1, Pallas kernels, count_words(): pl.pallas_call(words_kernel, grid=(nets // WIDE,), out_shape=jax.ShapeDty...  8.86 us
    all_to_all x1, waiting for transfers between devices, summed_gram(): plane = jnp.sum(lax.all_to_all(copies, 'narrow', 0, 0), axis=0)  7.49 us
    all_gather x1, blocking collectives, summed_gram(): return lax.all_gather(share, 'wide', axis_index_groups=pairs, tiled=True)  4.86 us
    pallas_call x1, Pallas kernels, factor_and_embed(): pl.pallas_call(functools.partial(factor_kernel, scale), out_shape=(jax.Sh...  4.75 us
  transfers between devices with their start and end apart: 3, of which 1 were waited for; matrix products, arithmetic and copies ran while one was open for 0% of the time, Pallas kernels for 8%

profile of v5, /device:TPU:1, one launch (start us, length us, event | category | flops | bytes accessed | tf_op | source)
XLA Modules:
  0.0 107.3 jit_solution(13061131136846276995)
XLA Ops:
  0.6 4.7 %shard_map.60 = (bf16[64,1024]{1,0:T(8,128)(2,1)}, bf16[64,1024]{1,0:T(8,128)(2,1)}) custom-call(s32[2,1024]{1,0:T(2,128)} %rows_ref.1, bf16[64,4096]{1,0:T(8,128)(2,1)} %vectors_ref.3), custom_call_target="tpu_custom_call" | custom-call | flops 1073741824 | bytes 524288 | tf_op jit(solution)/shard_map/pallas_call | solution.py:60
  5.4 3.9 %collective-permute-start = (bf16[64,1024]{1,0:T(8,128)(2,1)}, bf16[64,1024]{1,0:T(8,128)(2,1)S(1)}, u32[]{:S(2)}, u32[]{:S(2)}) collective-permute-start(bf16[64,1024]{1,0:T(8,128)(2,1)} %get-tuple-element.6), channel_id=1, source_target_pairs={{0,1},{1,2},{2,3},{3,4},{4,5},{5,6},{6,7},{7,8},{8,9},{9,10},{10,1... | collective-permute-start | bytes 393224 | tf_op jit(solution)/shard_map/ppermute | solution.py:25
  9.3 6.2 %collective-permute-start.1 = (bf16[64,1024]{1,0:T(8,128)(2,1)}, bf16[64,1024]{1,0:T(8,128)(2,1)S(1)}, u32[]{:S(2)}, u32[]{:S(2)}) collective-permute-start(bf16[64,1024]{1,0:T(8,128)(2,1)} %get-tuple-element.7), channel_id=1, source_target_pairs={{0,511},{1,0},{2,1},{3,2},{4,3},{5,4},{6,5},{7,6},{8,7},{9,8},{10,... | collective-permute-start | bytes 393224 | tf_op jit(solution)/shard_map/ppermute | solution.py:25
  15.5 8.9 %shard_map.59.words_ref = s16[768,5120]{1,0:T(8,128)(2,1)} custom-call(s32[8,5120]{1,0:T(8,128)} %pins_ref.3), custom_call_target="tpu_custom_call" | custom-call | flops 94371840 | bytes 7864320 | tf_op jit(solution)/shard_map/pallas_call | solution.py:129
  24.4 0.0 collective-permute-done.prev_ref
  24.4 0.0 copy-start
  24.4 0.0 collective-permute-done.1.next_ref
  24.4 0.0 copy-start.1
  24.4 0.6 copy-done
  25.0 0.1 copy-done.1
  25.1 29.7 %shard_map.61 = (f32[64,4096]{1,0:T(8,128)}, f32[16,32,128]{2,1,0:T(8,128)}) custom-call(s16[768,5120]{1,0:T(8,128)(2,1)} %shard_map.59.words_ref, s32[8,5120]{1,0:T(8,128)} %pins_ref.3, bf16[64,4096]{1,0:T(8,128)(2,1)} %vectors_ref.3, bf16[64,1024]{1,0:T(8,128)(2,1)} %copy-done, bf16[64,1024]{1,0:T(8,128)(2,1)} %copy-done.1, f32[1,4096]{1,0:T(1,128)} %bitcast.3), custom_call_target="tpu_custom_call" | custom-call | tf_op jit(solution)/shard_map/pallas_call | solution.py:269
  54.8 3.5 %all-to-all-start = ((f32[16,32,128]{2,1,0:T(8,128)}), f32[16,32,128]{2,1,0:T(8,128)S(1)}, u32[]{:S(2)}, u32[]{:S(2)}) async-start(f32[16,32,128]{2,1,0:T(8,128)} %get-tuple-element.8), calls=%async_computation | async-start | bytes 524288 | tf_op jit(solution)/shard_map/all_to_all | solution.py:301
  58.3 7.5 %all-to-all-done = f32[16,32,128]{2,1,0:T(8,128)S(1)} async-done(((f32[16,32,128]{2,1,0:T(8,128)}), f32[16,32,128]{2,1,0:T(8,128)S(1)}, u32[]{:S(2)}, u32[]{:S(2)}) %all-to-all-start) | async-done | bytes 262176 | tf_op jit(solution)/shard_map/all_to_all | solution.py:301
  65.8 11.4 %all-gather = f32[64,128]{1,0:T(8,128)S(1)} all-gather(f32[32,128]{1,0:T(8,128)S(1)} %reduce_sum.27), channel_id=2, replica_groups={{0,16},{32,48},{64,80},{96,112},{128,144},{160,176},{192,208},{224,240}..., dimensions={0}, use_global_device_ids=true | all-gather | bytes 49152 | tf_op jit(solution)/shard_map/all_gather | solution.py:302
  77.3 20.4 %all_to_all.10 = f32[16,16,128]{2,1,0:T(8,128)S(1)} all-to-all(f32[16,16,128]{2,1,0:T(8,128)S(1)} %broadcast_in_dim.10), channel_id=1, replica_groups={{0,32,64,96,128,160,192,224,256,288,320,352,384,416,448,480},{16,48,80,..., dimensions={0} | all-to-all | bytes 262144 | tf_op jit(solution)/shard_map/all_to_all | solution.py:307
  97.7 4.9 %all_gather.11.gram_ref = f32[32,128]{1,0:T(8,128)} all-gather(f32[16,128]{1,0:T(8,128)S(1)} %reduce_sum.29), channel_id=1, replica_groups={{0,16},{32,48},{64,80},{96,112},{128,144},{160,176},{192,208},{224,240}..., dimensions={0}, use_global_device_ids=true | all-gather | bytes 24576 | tf_op jit(solution)/shard_map/all_gather | solution.py:308
  102.6 4.7 %shard_map.62 = (f32[64,4096]{1,0:T(8,128)}, f32[64,64]{1,0:T(8,128)}) custom-call(f32[32,128]{1,0:T(8,128)} %all_gather.11.gram_ref, f32[64,4096]{1,0:T(8,128)} %get-tuple-element.9.image_ref), custom_call_target="tpu_custom_call" | custom-call | tf_op jit(solution)/shard_map/pallas_call | solution.py:349
  (5 shorter events, 0.1 us)
Async XLA Ops:
  5.4 19.0 %collective-permute-start = (bf16[64,1024]{1,0:T(8,128)(2,1)}, bf16[64,1024]{1,0:T(8,128)(2,1)S(1)}, u32[]{:S(2)}, u32[]{:S(2)}) collective-permute-start(bf16[64,1024]{1,0:T(8,128)(2,1)} %get-tuple-element.6), channel_id=1, source_target_pairs={{0,1},{1,2},{2,3},{3,4},{4,5},{5,6},{6,7},{7,8},{8,9},{9,10},{10,1... | collective-permute-start | bytes 393224 | tf_op jit(solution)/shard_map/ppermute | solution.py:25
  9.3 15.1 %collective-permute-start.1 = (bf16[64,1024]{1,0:T(8,128)(2,1)}, bf16[64,1024]{1,0:T(8,128)(2,1)S(1)}, u32[]{:S(2)}, u32[]{:S(2)}) collective-permute-start(bf16[64,1024]{1,0:T(8,128)(2,1)} %get-tuple-element.7), channel_id=1, source_target_pairs={{0,511},{1,0},{2,1},{3,2},{4,3},{5,4},{6,5},{7,6},{8,7},{9,8},{10,... | collective-permute-start | bytes 393224 | tf_op jit(solution)/shard_map/ppermute | solution.py:25
  24.4 0.7 copy-start
  24.4 0.7 copy-start.1
  54.8 11.0 %all-to-all-start = ((f32[16,32,128]{2,1,0:T(8,128)}), f32[16,32,128]{2,1,0:T(8,128)S(1)}, u32[]{:S(2)}, u32[]{:S(2)}) async-start(f32[16,32,128]{2,1,0:T(8,128)} %get-tuple-element.8), calls=%async_computation | async-start | bytes 524288 | tf_op jit(solution)/shard_map/all_to_all | solution.py:301
